TPU v7x, 32 devices: a whole 2x2x4 slice. The times are simulated.
32 devices in a mesh: scan: 16 (over z, y, x), mode: 2 (over core).
Axes of the slice: x: 2, y: 2, z: 4, core: 2. Of those that a mesh axis runs over, the one named last changes fastest.
Arguments:
- object_field: float32 [2, 640, 1152], P(None, 'scan'), may hold values from -4.5 to 4.5
- probe: float32 [8, 2, 512, 512], P('mode'), may hold values from -1.5 to 1.5
- amplitude: float32 [16, 512, 512], P('scan'), may hold values from 0.2 to 1.8
- pos_row: int32 [16], P('scan'), may hold values from 0 to 128, as said below
- pos_col: int32 [16], P('scan'), may hold values from 0 to 640, as said below
- strip_of: int32 [16], P('scan'), may hold values from 0 to 15, each once
Outputs:
- object_grad: float32 [2, 640, 1152], P(None, 'scan')
- probe_grad: float32 [8, 2, 512, 512], P('mode')
Inputs may be any that keep to these rules, and one draw needn't show every extreme that they name: Pattern p covers object rows pos_row[p] to pos_row[p] + 511; the smallest and the largest allowed value both occur. Pattern p covers object columns pos_col[p] to pos_col[p] + 511; the smallest and the largest allowed value both occur.
All inputs are finite; a program needn't handle non-finite values.
Results may differ from a plain program's by a relative error of at most 0.0055.
The roundings to bfloat16 on the way count: a program that leaves them out, or rounds other values in their place, can miss the bound.
Values may be sent and summed in bfloat16 or wider, within the bound.
A program may use at most 128 MiB of HBM per device.

v0:
```python
import math

import jax
import jax.numpy as jnp
import numpy as np
from jax import lax
from jax.experimental import pallas as pl
from jax.experimental.pallas import tpu as pltpu
from jax.sharding import PartitionSpec as P

F32 = jnp.float32
BF16 = jnp.bfloat16
LANES = 128
META = 8
PLANE = 4
TILE = 256
PARAMS = pltpu.CompilerParams(vmem_limit_bytes=56 * 1024 * 1024)
VMEM = pl.BlockSpec(memory_space=pltpu.VMEM)
SMEM = pl.BlockSpec(memory_space=pltpu.SMEM)


def dft_tables(size):
    positions = np.arange(size, dtype=np.int32)
    angles = (positions[:, None] * positions[None, :] % size).astype(np.float32)
    angles = angles * np.float32(2.0 * math.pi / size)
    norm = np.float32(1.0 / math.sqrt(size))
    cosine, sine = np.cos(angles) * norm, np.sin(angles) * norm
    forward = np.block([[cosine, sine], [-sine, cosine]])
    inverse = np.block([[cosine, -sine], [sine, cosine]])
    return jnp.asarray(forward, BF16), jnp.asarray(inverse, BF16)


def gather_kernel(mine, out, line_send, line_recv, plane_send, plane_recv, swap_send, swap_recv):
    count = out.shape[1]
    lines = count // PLANE
    scan, mode = lax.axis_index("scan"), lax.axis_index("mode")
    line, place = scan // PLANE, lax.rem(scan, PLANE)
    in_line = [(lax.rem(line + k, lines) * PLANE + place, mode) for k in range(1, lines)]
    in_plane = [(line * PLANE + lax.rem(place + t, PLANE), mode) for t in range(1, PLANE)]
    partner = (scan, 1 - mode)

    barrier = pltpu.get_barrier_semaphore()
    for peer in in_line + in_plane + [partner]:
        pl.semaphore_signal(barrier, inc=1, device_id=peer, device_id_type=pl.DeviceIdType.MESH)
    pl.semaphore_wait(barrier, len(in_line) + len(in_plane) + 1)

    def push(src, dst, send, recv, peer):
        copy = pltpu.make_async_remote_copy(
            src_ref=src,
            dst_ref=dst,
            send_sem=send,
            recv_sem=recv,
            device_id=peer,
            device_id_type=pl.DeviceIdType.MESH,
        )
        copy.start()
        return copy

    own = out.at[mode, scan]
    line_copies = [
        push(mine, own, line_send.at[k], line_recv.at[k], peer) for k, peer in enumerate(in_line)
    ]
    plane_copies = [
        push(mine, own, plane_send.at[0, t], plane_recv.at[0, t], peer) for t, peer in enumerate(in_plane)
    ]
    out[mode, scan] = mine[...]
    for k, arriving in enumerate(line_copies):
        arriving.wait_recv()
        piece = out.at[mode, lax.rem(line + lines - k - 1, lines) * PLANE + place]
        plane_copies += [
            push(piece, piece, plane_send.at[k + 1, t], plane_recv.at[k + 1, t], peer)
            for t, peer in enumerate(in_plane)
        ]
    for copy in plane_copies:
        copy.wait_recv()
    last = push(out.at[mode], out.at[mode], swap_send, swap_recv, partner)
    for copy in line_copies + plane_copies:
        copy.wait_send()
    last.wait()


def cut_kernel(strips, row, col, held, patch, window):
    count, rows = held.shape[1], held.shape[2] - META
    size, cols = patch.shape[-1], held.shape[-1]
    wide = size + LANES

    def place(j, carry):
        at = pl.ds(pl.multiple_of(strips[j] * rows, 8), rows)
        for c in range(2):
            window[c, at, :cols] = held[c, j].astype(F32)[:rows]
        return carry

    lax.fori_loop(0, count, place, 0)
    across = pl.ds(pl.multiple_of(col[0] // LANES * LANES, LANES), wide)
    back = lax.rem(wide - lax.rem(col[0], LANES), wide)
    up = lax.rem(72 - lax.rem(row[0], 8), 72)
    for c in range(2):

        def cut(i, carry, c=c):
            block = window[c, pl.ds(pl.multiple_of(row[0] // 8 * 8 + i * 64, 8), 72), across]
            block = pltpu.roll(block, up, 0)[:64]
            patch[c, pl.ds(pl.multiple_of(i * 64, 64), 64), :] = pltpu.roll(block, back, 1)[:, :size]
            return carry

        lax.fori_loop(0, size // 64, cut, 0)


def forward_kernel(probe, patch, left, right, far, power, wave, half):
    size = patch.shape[-1]

    def leave(i, carry):
        at = pl.ds(pl.multiple_of(i * 64, 64), 64)
        low = pl.ds(pl.multiple_of(size + i * 64, 64), 64)
        pr, pi, xr, xi = probe[0, 0, at], probe[0, 1, at], patch[0, at], patch[1, at]
        wave[at] = (pr * xr - pi * xi).astype(BF16)
        wave[low] = (pr * xi + pi * xr).astype(BF16)
        return carry

    lax.fori_loop(0, size // 64, leave, 0)
    rows_product(left, wave, half)
    first = pl.program_id(0) == 0

    def across(i, carry):
        at = pl.ds(pl.multiple_of(i * TILE, TILE), TILE)
        both = jnp.dot(half[at], right[...], preferred_element_type=F32)
        re, im = both[:, :size], both[:, size:]
        far[0, 0, at] = re
        far[0, 1, at] = im
        here = re * re + im * im
        power[at] = jnp.where(first, here, power[at] + here)
        return carry

    lax.fori_loop(0, size // TILE, across, 0)


def rows_product(left, wave, half):
    size = wave.shape[-1]
    for c in range(2):

        def down(i, carry, c=c):
            at = pl.ds(pl.multiple_of(c * size + i * TILE, TILE), TILE)
            to = pl.ds(pl.multiple_of(i * TILE, TILE), TILE)
            product = jnp.dot(left[at], wave[...], preferred_element_type=F32)
            half[to, c * size : (c + 1) * size] = product.astype(BF16)
            return carry

        lax.fori_loop(0, size // TILE, down, 0)


def backward_kernel(far, probe, patch, measured, power, left, right, term, grad, scale, wave, half):
    size = patch.shape[-1]
    first = pl.program_id(0) == 0

    @pl.when(first)
    def _():
        total = jnp.maximum(power[...], 0.25)
        scale[...] = 1.0 - measured[...] / jnp.sqrt(total)

    def residual(i, carry):
        at = pl.ds(pl.multiple_of(i * 64, 64), 64)
        low = pl.ds(pl.multiple_of(size + i * 64, 64), 64)
        wave[at] = (far[0, 0, at] * scale[at]).astype(BF16)
        wave[low] = (far[0, 1, at] * scale[at]).astype(BF16)
        return carry

    lax.fori_loop(0, size // 64, residual, 0)
    rows_product(left, wave, half)

    def across(i, carry):
        at = pl.ds(pl.multiple_of(i * TILE, TILE), TILE)
        both = jnp.dot(half[at], right[...], preferred_element_type=F32)
        br, bi = both[:, :size], both[:, size:]
        pr, pi, xr, xi = probe[0, 0, at], probe[0, 1, at], patch[0, at], patch[1, at]
        term[0, 0, at] = (xr * br + xi * bi).astype(BF16)
        term[0, 1, at] = (xr * bi - xi * br).astype(BF16)
        re, im = pr * br + pi * bi, pr * bi - pi * br
        grad[0, at] = jnp.where(first, re, grad[0, at] + re)
        grad[1, at] = jnp.where(first, im, grad[1, at] + im)
        return carry

    lax.fori_loop(0, size // TILE, across, 0)


def place_kernel(strips, row, grad, out, padded):
    count, parts, rows, size = out.shape
    padded[...] = jnp.zeros_like(padded)
    padded[:, rows : rows + size, :] = grad[...]

    def one(j, carry):
        start = jnp.clip(strips[j] * rows - row[0], -rows, size) + rows
        base = pl.ds(pl.multiple_of(start // 8 * 8, 8), rows + 8)
        up = lax.rem(rows + 8 - lax.rem(start, 8), rows + 8)
        for k in range(parts):
            out[j, k] = pltpu.roll(padded[k, base, :], up, 0)[:rows]
        return carry

    lax.fori_loop(0, count, one, 0)


def add_kernel(cols, received, out, total):
    count, parts, rows, size = received.shape
    total[...] = jnp.zeros_like(total)
    edge = jnp.zeros((rows, LANES), F32)

    def one(j, carry):
        across = pl.ds(pl.multiple_of(cols[j] // LANES * LANES, LANES), size + LANES)
        shift = lax.rem(cols[j], LANES)
        for k in range(parts):
            piece = jnp.concatenate([received[j, k], edge], axis=1)
            total[k, :, across] += pltpu.roll(piece, shift, 1)
        return carry

    lax.fori_loop(0, count, one, 0)
    out[...] = total[:, :, : out.shape[-1]]


def shards(object_field, probe, amplitude, pos_row, pos_col, strip_of):
    size = probe.shape[-1]
    modes = probe.shape[0]
    rows, cols = object_field.shape[1], object_field.shape[2]
    devices, groups = lax.axis_size("scan"), lax.axis_size("mode")
    padded_cols = cols + LANES
    forward, inverse = dft_tables(size)

    def swap(x):
        return lax.ppermute(x, "mode", [(0, 1), (1, 0)])

    lane = lax.broadcasted_iota(jnp.int32, (2, META, cols), 2)
    numbers = jnp.where(lane == 0, strip_of[0], jnp.where(lane == 1, pos_col[0] // LANES, pos_col[0] % LANES))
    packed = jnp.concatenate([object_field.astype(BF16), numbers.astype(BF16)], axis=1)
    me = lax.axis_index("mode")
    if groups == 2 and devices % PLANE == 0:
        dma, lines = pltpu.SemaphoreType.DMA, devices // PLANE
        held = pl.pallas_call(
            gather_kernel,
            out_shape=jax.ShapeDtypeStruct((2, devices, rows + META, cols), BF16),
            in_specs=[VMEM],
            out_specs=VMEM,
            scratch_shapes=[
                dma((max(lines - 1, 1),)),
                dma((max(lines - 1, 1),)),
                dma((lines, PLANE - 1)),
                dma((lines, PLANE - 1)),
                dma,
                dma,
            ],
            compiler_params=pltpu.CompilerParams(
                vmem_limit_bytes=56 * 1024 * 1024, collective_id=0, has_side_effects=True
            ),
        )(lax.dynamic_index_in_dim(packed, me, 0, keepdims=False))
    else:
        held = lax.all_gather(packed, "scan", axis=1)
    numbers = held[0, :, rows, :3].astype(jnp.int32)
    strips = numbers[:, 0]
    all_cols = numbers[:, 1] * LANES + numbers[:, 2]

    wave_shape = jax.ShapeDtypeStruct((2, size, size), F32)
    patch = pl.pallas_call(
        cut_kernel,
        out_shape=wave_shape,
        in_specs=[SMEM, SMEM, SMEM, VMEM],
        out_specs=VMEM,
        scratch_shapes=[pltpu.VMEM((2, devices * rows + 8, padded_cols), F32)],
        compiler_params=PARAMS,
    )(strips, pos_row, pos_col, held)

    def whole(*shape):
        return pl.BlockSpec(shape, lambda m: (0,) * len(shape))

    mode_spec = pl.BlockSpec((1, 2, size, size), lambda m: (m, 0, 0, 0))
    table_spec = whole(2 * size, 2 * size)
    buffers = [pltpu.VMEM((2 * size, size), BF16), pltpu.VMEM((size, 2 * size), BF16)]
    far, power = pl.pallas_call(
        forward_kernel,
        grid=(modes,),
        out_shape=(
            jax.ShapeDtypeStruct((modes, 2, size, size), F32),
            jax.ShapeDtypeStruct((size, size), F32),
        ),
        in_specs=[mode_spec, whole(2, size, size), table_spec, table_spec],
        out_specs=(mode_spec, whole(size, size)),
        scratch_shapes=buffers,
        compiler_params=PARAMS,
    )(probe, patch, forward, inverse)
    power = power + swap(power) if groups == 2 else lax.psum(power, "mode")
    term, grad = pl.pallas_call(
        backward_kernel,
        grid=(modes,),
        out_shape=(jax.ShapeDtypeStruct((modes, 2, size, size), BF16), wave_shape),
        in_specs=[
            mode_spec,
            mode_spec,
            whole(2, size, size),
            whole(size, size),
            whole(size, size),
            table_spec,
            table_spec,
        ],
        out_specs=(mode_spec, whole(2, size, size)),
        scratch_shapes=[pltpu.VMEM((size, size), F32)] + buffers,
        compiler_params=PARAMS,
    )(far, probe, patch, amplitude[0], power, inverse, forward)
    probe_grad = lax.psum(term, "scan").astype(F32)

    if groups == 2:
        mine = lax.dynamic_index_in_dim(grad, me, 0, keepdims=True)
        other = lax.dynamic_index_in_dim(grad, 1 - me, 0, keepdims=True)
        grad = mine + swap(other)
    else:
        grad = lax.psum(grad, "mode")
    parts = grad.shape[0]
    pieces = pl.pallas_call(
        place_kernel,
        out_shape=jax.ShapeDtypeStruct((devices, parts, rows, size), F32),
        in_specs=[SMEM, SMEM, VMEM],
        out_specs=VMEM,
        scratch_shapes=[pltpu.VMEM((parts, size + 2 * rows + 8, size), F32)],
        compiler_params=PARAMS,
    )(strips, pos_row, grad)
    received = lax.all_to_all(pieces.astype(BF16), "scan", 0, 0, tiled=False).astype(F32)
    strip_grad = pl.pallas_call(
        add_kernel,
        out_shape=jax.ShapeDtypeStruct((parts, rows, cols), F32),
        in_specs=[SMEM, VMEM],
        out_specs=VMEM,
        scratch_shapes=[pltpu.VMEM((parts, rows, padded_cols), F32)],
        compiler_params=PARAMS,
    )(all_cols, received)
    if groups == 2:
        theirs = swap(strip_grad)
        strip_grad = jnp.where(
            me == 0,
            jnp.concatenate([strip_grad, theirs]),
            jnp.concatenate([theirs, strip_grad]),
        )
    return (strip_grad, probe_grad)


def solution(mesh):
    return jax.shard_map(
        shards,
        mesh=mesh,
        in_specs=(
            P(None, "scan", None),
            P("mode", None, None, None),
            P("scan", None, None),
            P("scan"),
            P("scan"),
            P("scan"),
        ),
        out_specs=(P(None, "scan", None), P("mode", None, None, None)),
        check_vma=False,
    )
```

profile of v0, /device:TPU:0, one launch (start us, length us, event | category | flops | bytes accessed | tf_op | source)
XLA Modules:
  0.0 293.1 jit_solution(4892865350425346519)
XLA Ops:
  7.2 0.0 all-reduce.2.cloned.1.call-start
  7.9 1.0 convert_element_type.21
  9.6 0.7 fusion.1.mine
  10.3 32.3 %shard_map.95.held = bf16[2,16,48,1152]{3,2,1,0:T(8,128)(2,1)} custom-call(bf16[48,1152]{1,0:T(8,128)(2,1)} %fusion.1.mine), custom_call_target="tpu_custom_call" | custom-call | tf_op jit(solution)/shard_map/pallas_call | solution.py:234
  42.6 0.8 slice_convert_fusion
  43.3 0.1 copy.11
  43.4 0.6 slice_bitcast_fusion
  44.7 6.0 %shard_map.96.patch = f32[2,512,512]{2,1,0:T(8,128)} custom-call(s32[16]{0:T(128)} %get-tuple-element.10.strips, s32[1]{0:T(128)S(6)} %copy.13.row, s32[1]{0:T(128)} %copy.14.col, bf16[2,16,48,1152]{3,2,1,0:T(8,128)(2,1)} %shard_map.95.held), custom_call_target="tpu_custom_call" | custom-call | tf_op jit(solution)/shard_map/pallas_call | solution.py:258
  50.7 19.2 %shard_map.97 = (f32[4,2,512,512]{3,2,1,0:T(8,128)}, f32[512,512]{1,0:T(8,128)}) custom-call(f32[4,2,512,512]{3,2,1,0:T(8,128)} %probe.3, f32[2,512,512]{2,1,0:T(8,128)} %shard_map.96.patch, bf16[1024,1024]{1,0:T(8,128)(2,1)} %constant.52.clone.left.right, bf16[1024,1024]{1,0:T(8,128)(2,1)} %constant.53.clone.right.left), custom_call_target="tpu_custom_call" | custom-call | tf_op jit(solution)/shard_map/pallas_call | solution.py:273
  69.9 0.4 collective-permute-start
  70.3 2.5 collective-permute-done
  72.8 2.4 add.32.power
  75.2 22.6 %shard_map.98 = (bf16[4,2,512,512]{3,2,1,0:T(8,128)(2,1)}, f32[2,512,512]{2,1,0:T(8,128)}) custom-call(f32[4,2,512,512]{3,2,1,0:T(8,128)} %get-tuple-element.6.far, f32[4,2,512,512]{3,2,1,0:T(8,128)} %probe.3, f32[2,512,512]{2,1,0:T(8,128)} %shard_map.96.patch, f32[512,512]{1,0:T(8,128)} %bitcast.15, f32[512,512]{1,0:T(8,128)} %add.32.power, ...), custom_call_target="tpu_custom_call" | custom-call | tf_op jit(solution)/shard_map/pallas_call | solution.py:286
  97.8 0.0 copy-start
  97.8 0.0 all-reduce.2.cloned.1.call-update
  97.8 1.6 copy-done
  99.4 0.1 constant_dynamic-slice_fusion
  99.5 0.4 collective-permute-start.1
  99.9 2.3 collective-permute-done.1
  102.2 1.3 dynamic-slice_add_fusion.grad
  103.4 3.1 %shard_map.99 = f32[16,1,40,512]{3,2,1,0:T(8,128)} custom-call(s32[16]{0:T(128)} %get-tuple-element.10.strips, s32[1]{0:T(128)S(6)} %copy.13.row, f32[1,512,512]{2,1,0:T(8,128)} %dynamic-slice_add_fusion.grad), custom_call_target="tpu_custom_call" | custom-call | tf_op jit(solution)/shard_map/pallas_call | solution.py:312
  106.5 1.4 convert_element_type.25
  107.9 41.3 %all_to_all.5 = bf16[16,1,40,512]{3,2,1,0:T(8,128)(2,1)S(1)} all-to-all(bf16[16,1,40,512]{3,2,1,0:T(8,128)(2,1)S(1)} %convert_element_type.25), channel_id=1, replica_groups=mesh['scan'=16,'mode'=2] {'scan'}, dimensions={0} | all-to-all | bytes 1310720 | tf_op jit(solution)/shard_map/all_to_all | solution.py:320
  149.2 1.2 convert_element_type.26.received
  150.5 3.9 %shard_map.100 = f32[1,40,1152]{2,1,0:T(8,128)} custom-call(s32[16]{0:T(128)} %get-tuple-element.11.cols, f32[16,1,40,512]{3,2,1,0:T(8,128)} %convert_element_type.26.received), custom_call_target="tpu_custom_call" | custom-call | tf_op jit(solution)/shard_map/pallas_call | solution.py:321
  154.3 0.0 collective-permute-start.2
  154.3 1.6 collective-permute-done.2
  156.0 1.8 maximum_select_fusion
  157.7 121.8 %all-reduce.2.cloned.1.call-done = bf16[4,2,512,512]{3,2,1,0:T(8,128)(2,1)} async-done(((bf16[4,2,512,512]{3,2,1,0:T(8,128)(2,1)}), bf16[4,2,512,512]{3,2,1,0:T(8,128)(2,1)}) %all-reduce.2.cloned.1.call-update) | async-done | bytes 4194320 | tf_op jit(solution)/shard_map/psum | solution.py:303
  279.5 6.7 %convert_element_type.27 = f32[4,2,512,512]{3,2,1,0:T(8,128)} convert(bf16[4,2,512,512]{3,2,1,0:T(8,128)(2,1)} %all-reduce.2.cloned.1.call-done) | non-fusion elementwise | flops 2097152 | bytes 12582912 | tf_op jit(solution)/shard_map/convert_element_type | solution.py:303
  (3 shorter events, 0.0 us)
Async XLA Ops:
  7.2 272.3 %all-reduce.2.cloned.1.call-start = ((), (), s32[]{:S(2)}) async-start(), calls=%async_computation.1 | async-start | bytes 8388608 | tf_op jit(solution)/shard_map/psum | solution.py:303
  69.9 2.9 collective-permute-start
  97.8 1.6 copy-start
  99.5 2.7 collective-permute-start.1
  154.3 1.6 collective-permute-start.2
Sparse Core Ops, SparseCore 0:
  97.9 181.5 all-reduce.1
where the time goes:
time: 294 us; the launch traced here: 293 us
  waiting for transfers between devices  128 us (44%)
  Pallas kernels  87 us (30%)
  blocking collectives  41.3 us (14%)
  other arithmetic  17.9 us (6%)
  between operations  16.1 us (5%)
    psum x1, waiting for transfers between devices, shards(): probe_grad = lax.psum(term, 'scan').astype(F32)  122 us
    all_to_all x1, blocking collectives, shards(): lax.all_to_all(pieces.astype(BF16), 'scan', 0, 0, tiled=False).astype(F32)  41.3 us
    pallas_call x1, Pallas kernels, shards(): pl.pallas_call(gather_kernel, out_shape=jax.ShapeDtypeStruct((2, devices,...  32.3 us
    pallas_call x1, Pallas kernels, shards(): pl.pallas_call(backward_kernel, grid=(modes,), out_shape=(jax.ShapeDtypeS...  22.6 us
    pallas_call x1, Pallas kernels, shards(): pl.pallas_call(forward_kernel, grid=(modes,), out_shape=(jax.ShapeDtypeSt...  19.2 us
    convert_element_type x1, other arithmetic, shards(): probe_grad = lax.psum(term, 'scan').astype(F32)  6.75 us
    ppermute x3, waiting for transfers between devices, swap(): return lax.ppermute(x, 'mode', [(0, 1), (1, 0)])  6.42 us
    pallas_call x1, Pallas kernels, shards(): pl.pallas_call(cut_kernel, out_shape=wave_shape, in_specs=[SMEM, SMEM, SM...  6 us
  transfers between devices with their start and end apart: 4, of which 4 were waited for; matrix products, arithmetic and copies ran while one was open for 2% of the time, Pallas kernels for 2%

commit v1 on v0

--- a/solution.py
+++ b/solution.py
@@ -17,6 +17,7 @@
 PARAMS = pltpu.CompilerParams(vmem_limit_bytes=56 * 1024 * 1024)
 VMEM = pl.BlockSpec(memory_space=pltpu.VMEM)
 SMEM = pl.BlockSpec(memory_space=pltpu.SMEM)
+MESH = pl.DeviceIdType.MESH
 
 
 def dft_tables(size):
@@ -179,6 +180,208 @@
         return carry
 
     lax.fori_loop(0, size // TILE, across, 0)
+
+
+def mesh_peer(scan, mode, planes, dx, dy, dz):
+    z, y, x = scan // 4, lax.rem(scan // 2, 2), lax.rem(scan, 2)
+    x, y = lax.rem(x + dx, 2), lax.rem(y + dy, 2)
+    return (lax.rem(z + dz, planes) * 4 + y * 2 + x, mode)
+
+
+def core_kernel(
+    probe, patch, measured, left, right, result, grad,
+    far, power, power_in, scale, wave, half, term, got1, sum1, got2, sum2, got3,
+    swap_send, swap_recv, send, recv, send_z, recv_z, ship_z, land_z,
+):
+    modes, size = probe.shape[0], patch.shape[-1]
+    planes = got3.shape[2] + 1
+    scan, mode = lax.axis_index("scan"), lax.axis_index("mode")
+    z, y, x = scan // 4, lax.rem(scan // 2, 2), lax.rem(scan, 2)
+    partner = (scan, 1 - mode)
+    peer_x = mesh_peer(scan, mode, planes, 1, 0, 0)
+    peer_y = mesh_peer(scan, mode, planes, 0, 1, 0)
+    peers_z = [mesh_peer(scan, mode, planes, 0, 0, k) for k in range(1, planes)]
+    first_peer, second_peer = (peer_x, peer_y), (peer_y, peer_x)
+    first_at, second_at = (x, y), (y, x)
+    h, q, e = size // 2, size // 4, size // 4 // planes
+
+    barrier = pltpu.get_barrier_semaphore()
+    everyone = [partner, peer_x, peer_y] + peers_z
+    for peer in everyone:
+        pl.semaphore_signal(barrier, inc=1, device_id=peer, device_id_type=MESH)
+    pl.semaphore_wait(barrier, len(everyone))
+
+    def remote(src, dst, send_sem, recv_sem, peer):
+        return pltpu.make_async_remote_copy(
+            src_ref=src, dst_ref=dst, send_sem=send_sem, recv_sem=recv_sem, device_id=peer, device_id_type=MESH
+        )
+
+    def rows(start, count, step):
+        return pl.ds(pl.multiple_of(start, step), count)
+
+    def copy1(m, c):
+        away = rows((1 - first_at[c]) * h, h, h)
+        return remote(term.at[m, c, away], got1.at[m, c], send.at[0, m, c], recv.at[0, m, c], first_peer[c])
+
+    def copy2(m, c):
+        away = rows((1 - second_at[c]) * q, q, q)
+        return remote(sum1.at[m, c, away], got2.at[m, c], send.at[1, m, c], recv.at[1, m, c], second_peer[c])
+
+    def copy3(m, c, k):
+        away = rows(lax.rem(z + k, planes) * e, e, e)
+        return remote(
+            sum2.at[m, c, away], got3.at[m, c, k - 1], send_z.at[m, c, k - 1], recv_z.at[m, c, k - 1], peers_z[k - 1]
+        )
+
+    def base(c):
+        return first_at[c] * h + second_at[c] * q
+
+    def copy4(m, c, k):
+        own = result.at[m, c, rows(base(c) + z * e, e, e)]
+        return remote(own, own, ship_z.at[m, c, k - 1], land_z.at[m, c, k - 1], peers_z[k - 1])
+
+    def copy5(m, c):
+        own = result.at[m, c, rows(base(c), q, q)]
+        return remote(own, own, send.at[2, m, c], recv.at[2, m, c], second_peer[c])
+
+    def copy6(m, c):
+        own = result.at[m, c, rows(first_at[c] * h, h, h)]
+        return remote(own, own, send.at[3, m, c], recv.at[3, m, c], first_peer[c])
+
+    def start(stage, m):
+        for c in range(2):
+            if stage in (3, 4):
+                for k in range(1, planes):
+                    (copy3, copy4)[stage - 3](m, c, k).start()
+            else:
+                {1: copy1, 2: copy2, 5: copy5, 6: copy6}[stage](m, c).start()
+
+    def finish(stage, m):
+        for c in range(2):
+            if stage == 1:
+                copy1(m, c).wait_recv()
+                mine = term[m, c, rows(first_at[c] * h, h, h)].astype(F32)
+                sum1[m, c] = (mine + got1[m, c].astype(F32)).astype(BF16)
+            if stage == 2:
+                copy2(m, c).wait_recv()
+                mine = sum1[m, c, rows(second_at[c] * q, q, q)].astype(F32)
+                sum2[m, c] = (mine + got2[m, c].astype(F32)).astype(BF16)
+            if stage == 3:
+                total = sum2[m, c, rows(z * e, e, e)].astype(F32)
+                for k in range(1, planes):
+                    copy3(m, c, k).wait_recv()
+                    total = total + got3[m, c, k - 1].astype(F32)
+                result[m, c, rows(base(c) + z * e, e, e)] = total.astype(BF16)
+            if stage == 4:
+                for k in range(1, planes):
+                    copy4(m, c, k).wait_recv()
+            if stage == 5:
+                copy5(m, c).wait_recv()
+            if stage == 6:
+                copy6(m, c).wait_recv()
+
+    def swap(i):
+        at = rows(i * TILE, TILE, TILE)
+        return remote(power.at[at], power_in.at[at], swap_send.at[i], swap_recv.at[i], partner)
+
+    def product(table, source):
+        for c in range(2):
+
+            def down(i, carry, c=c):
+                at = rows(c * size + i * TILE, TILE, TILE)
+                out = jnp.dot(table[at], source[...], preferred_element_type=F32)
+                half[rows(i * TILE, TILE, TILE), c * size : (c + 1) * size] = out.astype(BF16)
+                return carry
+
+            lax.fori_loop(0, size // TILE, down, 0)
+
+    def forward(m, carry):
+        def leave(i, carry):
+            at, low = rows(i * 64, 64, 64), rows(size + i * 64, 64, 64)
+            pr, pi, xr, xi = probe[m, 0, at], probe[m, 1, at], patch[0, at], patch[1, at]
+            wave[at] = (pr * xr - pi * xi).astype(BF16)
+            wave[low] = (pr * xi + pi * xr).astype(BF16)
+            return carry
+
+        lax.fori_loop(0, size // 64, leave, 0)
+        product(left, wave)
+
+        def across(i, carry):
+            at = rows(i * TILE, TILE, TILE)
+            both = jnp.dot(half[at], right[...], preferred_element_type=F32)
+            re, im = both[:, :size], both[:, size:]
+            far[m, 0, at] = re
+            far[m, 1, at] = im
+            here = re * re + im * im
+            power[at] = jnp.where(m == 0, here, power[at] + here)
+
+            @pl.when(m == modes - 1)
+            def _():
+                swap(i).start()
+
+            return carry
+
+        lax.fori_loop(0, size // TILE, across, 0)
+        return carry
+
+    lax.fori_loop(0, modes, forward, 0)
+    for i in range(size // TILE):
+        at = pl.ds(i * TILE, TILE)
+        swap(i).wait_recv()
+        total = jnp.maximum(power[at] + power_in[at], 0.25)
+        scale[at] = 1.0 - measured[at] / jnp.sqrt(total)
+
+    def backward(m, carry):
+        def residual(i, carry):
+            at, low = rows(i * 64, 64, 64), rows(size + i * 64, 64, 64)
+            wave[at] = (far[m, 0, at] * scale[at]).astype(BF16)
+            wave[low] = (far[m, 1, at] * scale[at]).astype(BF16)
+            return carry
+
+        lax.fori_loop(0, size // 64, residual, 0)
+        product(right, wave)
+
+        def across(i, carry):
+            at = rows(i * TILE, TILE, TILE)
+            both = jnp.dot(half[at], left[...], preferred_element_type=F32)
+            br, bi = both[:, :size], both[:, size:]
+            pr, pi, xr, xi = probe[m, 0, at], probe[m, 1, at], patch[0, at], patch[1, at]
+            term[m, 0, at] = (xr * br + xi * bi).astype(BF16)
+            term[m, 1, at] = (xr * bi - xi * br).astype(BF16)
+            re, im = pr * br + pi * bi, pr * bi - pi * br
+            grad[0, at] = jnp.where(m == 0, re, grad[0, at] + re)
+            grad[1, at] = jnp.where(m == 0, im, grad[1, at] + im)
+            return carry
+
+        lax.fori_loop(0, size // TILE, across, 0)
+        start(1, m)
+
+        @pl.when(m >= 2)
+        def _():
+            finish(1, m - 2)
+            start(2, m - 2)
+
+        return carry
+
+    lax.fori_loop(0, modes, backward, 0)
+    steps = sorted((m + s, -s, m, s) for m in range(modes) for s in range(1, 7) if s > 1 or m >= modes - 2)
+    for _, _, m, s in steps:
+        finish(s, m)
+        if s < 6:
+            start(s + 1, m)
+
+    def drain(m, carry):
+        for c in range(2):
+            for copy in (copy1, copy2, copy5, copy6):
+                copy(m, c).wait_send()
+            for k in range(1, planes):
+                copy3(m, c, k).wait_send()
+                copy4(m, c, k).wait_send()
+        return carry
+
+    lax.fori_loop(0, modes, drain, 0)
+    for i in range(size // TILE):
+        swap(i).wait_send()
 
 
 def place_kernel(strips, row, grad, out, padded):
@@ -270,37 +473,74 @@
     mode_spec = pl.BlockSpec((1, 2, size, size), lambda m: (m, 0, 0, 0))
     table_spec = whole(2 * size, 2 * size)
     buffers = [pltpu.VMEM((2 * size, size), BF16), pltpu.VMEM((size, 2 * size), BF16)]
-    far, power = pl.pallas_call(
-        forward_kernel,
-        grid=(modes,),
-        out_shape=(
-            jax.ShapeDtypeStruct((modes, 2, size, size), F32),
-            jax.ShapeDtypeStruct((size, size), F32),
-        ),
-        in_specs=[mode_spec, whole(2, size, size), table_spec, table_spec],
-        out_specs=(mode_spec, whole(size, size)),
-        scratch_shapes=buffers,
-        compiler_params=PARAMS,
-    )(probe, patch, forward, inverse)
-    power = power + swap(power) if groups == 2 else lax.psum(power, "mode")
-    term, grad = pl.pallas_call(
-        backward_kernel,
-        grid=(modes,),
-        out_shape=(jax.ShapeDtypeStruct((modes, 2, size, size), BF16), wave_shape),
-        in_specs=[
-            mode_spec,
-            mode_spec,
-            whole(2, size, size),
-            whole(size, size),
-            whole(size, size),
-            table_spec,
-            table_spec,
-        ],
-        out_specs=(mode_spec, whole(2, size, size)),
-        scratch_shapes=[pltpu.VMEM((size, size), F32)] + buffers,
-        compiler_params=PARAMS,
-    )(far, probe, patch, amplitude[0], power, inverse, forward)
-    probe_grad = lax.psum(term, "scan").astype(F32)
+    planes = devices // 4
+    if groups == 2 and planes >= 2 and size % (64 * planes) == 0:
+        dma = pltpu.SemaphoreType.DMA
+        h, q, e = size // 2, size // 4, size // 4 // planes
+        term, grad = pl.pallas_call(
+            core_kernel,
+            out_shape=(jax.ShapeDtypeStruct((modes, 2, size, size), BF16), wave_shape),
+            in_specs=[VMEM] * 5,
+            out_specs=(VMEM, VMEM),
+            scratch_shapes=[
+                pltpu.VMEM((modes, 2, size, size), F32),
+                pltpu.VMEM((size, size), F32),
+                pltpu.VMEM((size, size), F32),
+                pltpu.VMEM((size, size), F32),
+                pltpu.VMEM((2 * size, size), BF16),
+                pltpu.VMEM((size, 2 * size), BF16),
+                pltpu.VMEM((modes, 2, size, size), BF16),
+                pltpu.VMEM((modes, 2, h, size), BF16),
+                pltpu.VMEM((modes, 2, h, size), BF16),
+                pltpu.VMEM((modes, 2, q, size), BF16),
+                pltpu.VMEM((modes, 2, q, size), BF16),
+                pltpu.VMEM((modes, 2, planes - 1, e, size), BF16),
+                dma((size // TILE,)),
+                dma((size // TILE,)),
+                dma((4, modes, 2)),
+                dma((4, modes, 2)),
+                dma((modes, 2, planes - 1)),
+                dma((modes, 2, planes - 1)),
+                dma((modes, 2, planes - 1)),
+                dma((modes, 2, planes - 1)),
+            ],
+            compiler_params=pltpu.CompilerParams(
+                vmem_limit_bytes=56 * 1024 * 1024, collective_id=1, has_side_effects=True
+            ),
+        )(probe, patch, amplitude[0], forward, inverse)
+        probe_grad = term.astype(F32)
+    else:
+        far, power = pl.pallas_call(
+            forward_kernel,
+            grid=(modes,),
+            out_shape=(
+                jax.ShapeDtypeStruct((modes, 2, size, size), F32),
+                jax.ShapeDtypeStruct((size, size), F32),
+            ),
+            in_specs=[mode_spec, whole(2, size, size), table_spec, table_spec],
+            out_specs=(mode_spec, whole(size, size)),
+            scratch_shapes=buffers,
+            compiler_params=PARAMS,
+        )(probe, patch, forward, inverse)
+        power = power + swap(power) if groups == 2 else lax.psum(power, "mode")
+        term, grad = pl.pallas_call(
+            backward_kernel,
+            grid=(modes,),
+            out_shape=(jax.ShapeDtypeStruct((modes, 2, size, size), BF16), wave_shape),
+            in_specs=[
+                mode_spec,
+                mode_spec,
+                whole(2, size, size),
+                whole(size, size),
+                whole(size, size),
+                table_spec,
+                table_spec,
+            ],
+            out_specs=(mode_spec, whole(2, size, size)),
+            scratch_shapes=[pltpu.VMEM((size, size), F32)] + buffers,
+            compiler_params=PARAMS,
+        )(far, probe, patch, amplitude[0], power, inverse, forward)
+        probe_grad = lax.psum(term, "scan").astype(F32)
 
     if groups == 2:
         mine = lax.dynamic_index_in_dim(grad, me, 0, keepdims=True)

time: 294 us -> 206 us (0.70)
  waiting for transfers between devices: 128 us -> 2.65 us
  Pallas kernels: 87 us -> 159 us
  blocking collectives: 41.3 us -> 25.4 us
  between operations: 16.1 us -> 2.7 us
  other arithmetic: 17.9 us -> 14.4 us
    psum x1 -> x0, waiting for transfers between devices: 122 us -> none  [shards(): probe_grad = lax.psum(term, 'scan').astype(F32)]
    pallas_call x2 -> x1, Pallas kernels: 41.8 us -> 114 us  [shards(): pl.pallas_call(core_kernel, out_shape=(jax.ShapeDtypeStruct((modes, 2, si...]
    all_to_all x1, blocking collectives: 41.3 us -> 25.4 us  [shards(): lax.all_to_all(pieces.astype(BF16), 'scan', 0, 0, tiled=False).astype(F32)]
    ppermute x3 -> x2, waiting for transfers between devices: 6.42 us -> 2.65 us  [swap(): return lax.ppermute(x, 'mode', [(0, 1), (1, 0)])]
  transfers between devices with their start and end apart: 4 -> 2, of which waited for: 4 -> 1; matrix products, arithmetic and copies ran while one was open for 2% -> 3% of each run, Pallas kernels for 2% -> 0%
where the time goes in v1:
time: 206 us
  Pallas kernels  159 us (77%)
  blocking collectives  25.4 us (12%)
  other arithmetic  14.4 us (7%)
  between operations  2.7 us (1%)
  waiting for transfers between devices  2.65 us (1%)
    pallas_call x1, Pallas kernels, shards(): pl.pallas_call(core_kernel, out_shape=(jax.ShapeDtypeStruct((modes, 2, si...  114 us
    pallas_call x1, Pallas kernels, shards(): pl.pallas_call(gather_kernel, out_shape=jax.ShapeDtypeStruct((2, devices,...  32.3 us
    all_to_all x1, blocking collectives, shards(): lax.all_to_all(pieces.astype(BF16), 'scan', 0, 0, tiled=False).astype(F32)  25.4 us
    convert_element_type x1, other arithmetic, shards(): probe_grad = term.astype(F32)  6.79 us
    pallas_call x1, Pallas kernels, shards(): pl.pallas_call(cut_kernel, out_shape=wave_shape, in_specs=[SMEM, SMEM, SM...  5.99 us
  transfers between devices with their start and end apart: 2, of which 1 were waited for; matrix products, arithmetic and copies ran while one was open for 3% of the time, Pallas kernels for 0%

profile of v1, /device:TPU:0, one launch (start us, length us, event | category | flops | bytes accessed | tf_op | source)
XLA Modules:
  0.0 205.9 jit_solution(685828576078706022)
XLA Ops:
  2.6 1.0 convert_element_type.21
  3.7 0.7 fusion.1.mine
  4.4 32.3 %shard_map.95.held = bf16[2,16,48,1152]{3,2,1,0:T(8,128)(2,1)} custom-call(bf16[48,1152]{1,0:T(8,128)(2,1)} %fusion.1.mine), custom_call_target="tpu_custom_call" | custom-call | tf_op jit(solution)/shard_map/pallas_call | solution.py:437
  36.6 0.8 slice_convert_fusion
  37.4 0.1 copy.11
  37.5 0.6 slice_bitcast_fusion
  38.1 6.0 %shard_map.96.patch = f32[2,512,512]{2,1,0:T(8,128)} custom-call(s32[16]{0:T(128)} %get-tuple-element.6.strips, s32[1]{0:T(128)S(6)} %copy.12.row, s32[1]{0:T(128)} %copy.13.col, bf16[2,16,48,1152]{3,2,1,0:T(8,128)(2,1)} %shard_map.95.held), custom_call_target="tpu_custom_call" | custom-call | tf_op jit(solution)/shard_map/pallas_call | solution.py:461
  44.1 114.0 %shard_map.97 = (bf16[4,2,512,512]{3,2,1,0:T(8,128)(2,1)}, f32[2,512,512]{2,1,0:T(8,128)}) custom-call(f32[4,2,512,512]{3,2,1,0:T(8,128)} %probe.1, f32[2,512,512]{2,1,0:T(8,128)} %shard_map.96.patch, f32[512,512]{1,0:T(8,128)} %bitcast.15, bf16[1024,1024]{1,0:T(8,128)(2,1)} %constant.52.clone.left, bf16[1024,1024]{1,0:T(8,128)(2,1)} %constant.53.clone.right), custom_call_target="tpu_custom_call" | custom-call | tf_op jit(solution)/shard_map/pallas_call | solution.py:480
  158.1 0.0 copy-start
  158.1 1.4 constant_dynamic-slice_fusion
  159.5 0.1 collective-permute-start
  159.6 2.6 %collective-permute-done = f32[1,512,512]{2,1,0:T(8,128)S(1)} collective-permute-done((f32[1,512,512]{2,1,0:T(8,128)S(1)}, f32[1,512,512]{2,1,0:T(8,128)S(1)}, u32[]{:S(2)}, u32[]{:S(2)}) %collective-permute-start) | collective-permute-done | bytes 1048608 | tf_op jit(solution)/shard_map/ppermute | solution.py:429
  162.3 0.0 copy-done
  162.3 1.2 dynamic-slice_add_fusion.grad
  163.4 3.0 %shard_map.98 = f32[16,1,40,512]{3,2,1,0:T(8,128)} custom-call(s32[16]{0:T(128)} %get-tuple-element.6.strips, s32[1]{0:T(128)S(6)} %copy.12.row, f32[1,512,512]{2,1,0:T(8,128)} %dynamic-slice_add_fusion.grad), custom_call_target="tpu_custom_call" | custom-call | tf_op jit(solution)/shard_map/pallas_call | solution.py:552
  166.5 1.4 convert_element_type.25
  167.9 25.4 %all_to_all.5 = bf16[16,1,40,512]{3,2,1,0:T(8,128)(2,1)S(1)} all-to-all(bf16[16,1,40,512]{3,2,1,0:T(8,128)(2,1)S(1)} %convert_element_type.25), channel_id=1, replica_groups=mesh['scan'=16,'mode'=2] {'scan'}, dimensions={0} | all-to-all | bytes 1310720 | tf_op jit(solution)/shard_map/all_to_all | solution.py:560
  193.3 1.2 convert_element_type.26.received
  194.5 3.9 %shard_map.99 = f32[1,40,1152]{2,1,0:T(8,128)} custom-call(s32[16]{0:T(128)} %get-tuple-element.7.cols, f32[16,1,40,512]{3,2,1,0:T(8,128)} %convert_element_type.26.received), custom_call_target="tpu_custom_call" | custom-call | tf_op jit(solution)/shard_map/pallas_call | solution.py:561
  198.4 0.0 collective-permute-start.1
  198.4 0.0 copy-start.1
  198.4 6.8 %convert_element_type.27 = f32[4,2,512,512]{3,2,1,0:T(8,128)} convert(bf16[4,2,512,512]{3,2,1,0:T(8,128)(2,1)} %get-tuple-element.5) | non-fusion elementwise | flops 2097152 | bytes 12582912 | tf_op jit(solution)/shard_map/convert_element_type | solution.py:511
  205.2 0.0 collective-permute-done.1
  205.2 0.0 copy-done.1
  205.2 0.8 maximum_select_fusion
  (3 shorter events, 0.0 us)
Async XLA Ops:
  158.1 4.2 %copy-start = (f32[2,512,512]{2,1,0:T(8,128)S(1)}, f32[2,512,512]{2,1,0:T(8,128)}, u32[]{:S(2)}) copy-start(f32[2,512,512]{2,1,0:T(8,128)} %get-tuple-element.4) | copy-start | bytes 6291460
  159.5 2.7 %collective-permute-start = (f32[1,512,512]{2,1,0:T(8,128)S(1)}, f32[1,512,512]{2,1,0:T(8,128)S(1)}, u32[]{:S(2)}, u32[]{:S(2)}) collective-permute-start(f32[1,512,512]{2,1,0:T(8,128)S(1)} %constant_dynamic-slice_fusion), channel_id=1, source_target_pairs={{0,1},{1,0},{2,3},{3,2},{4,5},{5,4},{6,7},{7,6},{8,9},{9,8},{10,11... | collective-permute-start | bytes 3145736 | tf_op jit(solution)/shard_map/ppermute | solution.py:429
  198.4 6.8 %collective-permute-start.1 = (f32[1,40,1152]{2,1,0:T(8,128)}, f32[1,40,1152]{2,1,0:T(8,128)S(1)}, u32[]{:S(2)}, u32[]{:S(2)}) collective-permute-start(f32[1,40,1152]{2,1,0:T(8,128)} %shard_map.99), channel_id=1, source_target_pairs={{0,1},{1,0},{2,3},{3,2},{4,5},{5,4},{6,7},{7,6},{8,9},{9,8},{10,11... | collective-permute-start | bytes 552968 | tf_op jit(solution)/shard_map/ppermute | solution.py:429
  198.4 6.8 %copy-start.1 = (f32[1,40,1152]{2,1,0:T(8,128)S(1)}, f32[1,40,1152]{2,1,0:T(8,128)}, u32[]{:S(2)}) copy-start(f32[1,40,1152]{2,1,0:T(8,128)} %shard_map.99) | copy-start | bytes 552964

commit v2 on v1

--- a/solution.py
+++ b/solution.py
@@ -189,11 +189,16 @@
 
 
 def core_kernel(
-    probe, patch, measured, left, right, result, grad,
+    strips, row, cols, probe_hbm, patch_hbm, measured_hbm, left_hbm, right_hbm, result, strip_grad,
+    probe, patch, measured, left, right,
     far, power, power_in, scale, wave, half, term, got1, sum1, got2, sum2, got3,
-    swap_send, swap_recv, send, recv, send_z, recv_z, ship_z, land_z,
+    grad, grad_in, summed, pieces, landed,
+    load, load_probe, swap_send, swap_recv, send, recv, send_z, recv_z, ship_z, land_z,
+    part_send, part_recv, piece_send, piece_recv, strip_send, strip_recv,
 ):
     modes, size = probe.shape[0], patch.shape[-1]
+    devices = lax.axis_size("scan")
+    strip, width = strip_grad.shape[1], strip_grad.shape[2]
     planes = got3.shape[2] + 1
     scan, mode = lax.axis_index("scan"), lax.axis_index("mode")
     z, y, x = scan // 4, lax.rem(scan // 2, 2), lax.rem(scan, 2)
@@ -206,9 +211,22 @@
     h, q, e = size // 2, size // 4, size // 4 // planes
 
     barrier = pltpu.get_barrier_semaphore()
-    everyone = [partner, peer_x, peer_y] + peers_z
+    everyone = [partner] + [(lax.rem(scan + k, devices), mode) for k in range(1, devices)]
     for peer in everyone:
         pl.semaphore_signal(barrier, inc=1, device_id=peer, device_id_type=MESH)
+
+    def probe_load(m):
+        return pltpu.make_async_copy(probe_hbm.at[m], probe.at[m], load_probe.at[m])
+
+    whole = [(patch_hbm, patch), (left_hbm, left), (right_hbm, right), (measured_hbm, measured)]
+    loads = [pltpu.make_async_copy(src, dst, load.at[i]) for i, (src, dst) in enumerate(whole)]
+    probe_load(0).start()
+    for copy in loads:
+        copy.start()
+    for m in range(1, modes):
+        probe_load(m).start()
+    for copy in loads:
+        copy.wait()
     pl.semaphore_wait(barrier, len(everyone))
 
     def remote(src, dst, send_sem, recv_sem, peer):
@@ -295,7 +313,81 @@
 
             lax.fori_loop(0, size // TILE, down, 0)
 
+    def part(i):
+        at = rows(i * TILE, TILE, TILE)
+        return remote(grad.at[1 - mode, at], grad_in.at[at], part_send.at[i], part_recv.at[i], partner)
+
+    deep = pieces.shape[0] // devices
+    mine = rows(scan * deep, deep, deep)
+
+    def one_hot(mask):
+        return jnp.where(mask, 1.0, 0.0).astype(BF16)
+
+    def piece(k):
+        to = lax.rem(scan + k, devices)
+        return remote(pieces.at[rows(to * deep, deep, deep)], landed.at[mine], piece_send.at[k - 1], piece_recv.at[k - 1], (to, mode))
+
+    def arrive(k):
+        come = lax.rem(scan + devices - k, devices)
+        at = rows(come * deep, deep, deep)
+        return remote(pieces.at[at], landed.at[at], piece_send.at[k - 1], piece_recv.at[k - 1], (come, mode))
+
+    def strip_swap():
+        return remote(strip_grad.at[mode], strip_grad.at[mode], strip_send, strip_recv, partner)
+
+    def cut_pieces():
+        for i in range(size // TILE):
+            part(i).wait_recv()
+            at = pl.ds(i * TILE, TILE)
+            summed[at] = (grad[mode, at] + grad_in[at]).astype(BF16)
+        ahead = lax.broadcasted_iota(jnp.int32, (deep, size), 1) - lax.broadcasted_iota(jnp.int32, (deep, size), 0)
+
+        def pick(j, carry):
+            wave[rows(j * deep, deep, deep)] = one_hot(ahead == strips[j] * strip - row[0])
+            return carry
+
+        lax.fori_loop(0, devices, pick, 0)
+
+        def move(i, carry):
+            at = rows(i * TILE, TILE, TILE)
+            pieces[at] = jnp.dot(wave[at], summed[...], preferred_element_type=F32).astype(BF16)
+            return carry
+
+        lax.fori_loop(0, devices * deep // TILE, move, 0)
+        for k in range(1, devices):
+            piece(k).start()
+        landed[mine] = pieces[mine]
+
+    def add_pieces():
+        for k in range(1, devices):
+            arrive(k).wait_recv()
+        strip_grad[mode] = jnp.zeros((strip, width), F32)
+        parts = size // LANES
+        ahead = lax.broadcasted_iota(jnp.int32, (LANES, 2 * LANES), 1)
+        ahead = ahead - lax.broadcasted_iota(jnp.int32, (LANES, 2 * LANES), 0)
+
+        def one(j, carry):
+            turn = one_hot(ahead == lax.rem(cols[j], LANES))
+            blocks = jnp.concatenate(
+                [landed[rows(j * deep, deep, deep), b * LANES : (b + 1) * LANES] for b in range(parts)]
+            )
+            moved = jnp.dot(blocks, turn, preferred_element_type=F32)
+            for b in range(parts + 1):
+                here = moved[b * deep : b * deep + strip, :LANES] if b < parts else 0.0
+                if b > 0:
+                    here = here + moved[(b - 1) * deep : (b - 1) * deep + strip, LANES:]
+                for t in range((width - size) // LANES + 1):
+                    if b + t < width // LANES:
+                        to = slice((b + t) * LANES, (b + t + 1) * LANES)
+                        strip_grad[mode, :, to] += jnp.where(cols[j] // LANES == t, here, 0.0)
+            return carry
+
+        lax.fori_loop(0, devices, one, 0)
+        strip_swap().start()
+
     def forward(m, carry):
+        probe_load(m).wait()
+
         def leave(i, carry):
             at, low = rows(i * 64, 64, 64), rows(size + i * 64, 64, 64)
             pr, pi, xr, xi = probe[m, 0, at], probe[m, 1, at], patch[0, at], patch[1, at]
@@ -351,6 +443,11 @@
             re, im = pr * br + pi * bi, pr * bi - pi * br
             grad[0, at] = jnp.where(m == 0, re, grad[0, at] + re)
             grad[1, at] = jnp.where(m == 0, im, grad[1, at] + im)
+
+            @pl.when(m == modes - 1)
+            def _():
+                part(i).start()
+
             return carry
 
         lax.fori_loop(0, size // TILE, across, 0)
@@ -365,7 +462,10 @@
 
     lax.fori_loop(0, modes, backward, 0)
     steps = sorted((m + s, -s, m, s) for m in range(modes) for s in range(1, 7) if s > 1 or m >= modes - 2)
+    cut_pieces()
     for _, _, m, s in steps:
+        if (m, s) == (1, 6):
+            add_pieces()
         finish(s, m)
         if s < 6:
             start(s + 1, m)
@@ -382,6 +482,10 @@
     lax.fori_loop(0, modes, drain, 0)
     for i in range(size // TILE):
         swap(i).wait_send()
+        part(i).wait_send()
+    for k in range(1, devices):
+        piece(k).wait_send()
+    strip_swap().wait()
 
 
 def place_kernel(strips, row, grad, out, padded):
@@ -473,28 +577,46 @@
     mode_spec = pl.BlockSpec((1, 2, size, size), lambda m: (m, 0, 0, 0))
     table_spec = whole(2 * size, 2 * size)
     buffers = [pltpu.VMEM((2 * size, size), BF16), pltpu.VMEM((size, 2 * size), BF16)]
-    planes = devices // 4
-    if groups == 2 and planes >= 2 and size % (64 * planes) == 0:
+    planes, deep = devices // 4, -(-rows // 16) * 16
+    fits = groups == 2 and devices == 4 * planes and planes >= 2 and size % (64 * planes) == 0
+    if fits and rows % 8 == 0 and devices * deep % TILE == 0 and devices * deep <= 2 * size:
         dma = pltpu.SemaphoreType.DMA
         h, q, e = size // 2, size // 4, size // 4 // planes
-        term, grad = pl.pallas_call(
+        vmem = pltpu.VMEM
+        any_space = pl.BlockSpec(memory_space=pl.ANY)
+        term, strip_grad = pl.pallas_call(
             core_kernel,
-            out_shape=(jax.ShapeDtypeStruct((modes, 2, size, size), BF16), wave_shape),
-            in_specs=[VMEM] * 5,
+            out_shape=(
+                jax.ShapeDtypeStruct((modes, 2, size, size), BF16),
+                jax.ShapeDtypeStruct((2, rows, cols), F32),
+            ),
+            in_specs=[SMEM] * 3 + [any_space] * 5,
             out_specs=(VMEM, VMEM),
             scratch_shapes=[
-                pltpu.VMEM((modes, 2, size, size), F32),
-                pltpu.VMEM((size, size), F32),
-                pltpu.VMEM((size, size), F32),
-                pltpu.VMEM((size, size), F32),
-                pltpu.VMEM((2 * size, size), BF16),
-                pltpu.VMEM((size, 2 * size), BF16),
-                pltpu.VMEM((modes, 2, size, size), BF16),
-                pltpu.VMEM((modes, 2, h, size), BF16),
-                pltpu.VMEM((modes, 2, h, size), BF16),
-                pltpu.VMEM((modes, 2, q, size), BF16),
-                pltpu.VMEM((modes, 2, q, size), BF16),
-                pltpu.VMEM((modes, 2, planes - 1, e, size), BF16),
+                vmem((modes, 2, size, size), F32),
+                vmem((2, size, size), F32),
+                vmem((size, size), F32),
+                vmem((2 * size, 2 * size), BF16),
+                vmem((2 * size, 2 * size), BF16),
+                vmem((modes, 2, size, size), F32),
+                vmem((size, size), F32),
+                vmem((size, size), F32),
+                vmem((size, size), F32),
+                vmem((2 * size, size), BF16),
+                vmem((size, 2 * size), BF16),
+                vmem((modes, 2, size, size), BF16),
+                vmem((modes, 2, h, size), BF16),
+                vmem((modes, 2, h, size), BF16),
+                vmem((modes, 2, q, size), BF16),
+                vmem((modes, 2, q, size), BF16),
+                vmem((modes, 2, planes - 1, e, size), BF16),
+                vmem((2, size, size), F32),
+                vmem((size, size), F32),
+                vmem((size, size), BF16),
+                vmem((devices * deep, size), BF16),
+                vmem((devices * deep, size), BF16),
+                dma((4,)),
+                dma((modes,)),
                 dma((size // TILE,)),
                 dma((size // TILE,)),
                 dma((4, modes, 2)),
@@ -503,44 +625,50 @@
                 dma((modes, 2, planes - 1)),
                 dma((modes, 2, planes - 1)),
                 dma((modes, 2, planes - 1)),
+                dma((size // TILE,)),
+                dma((size // TILE,)),
+                dma((devices - 1,)),
+                dma((devices - 1,)),
+                dma,
+                dma,
             ],
             compiler_params=pltpu.CompilerParams(
-                vmem_limit_bytes=56 * 1024 * 1024, collective_id=1, has_side_effects=True
+                vmem_limit_bytes=58 * 1024 * 1024, collective_id=1, has_side_effects=True
             ),
-        )(probe, patch, amplitude[0], forward, inverse)
-        probe_grad = term.astype(F32)
-    else:
-        far, power = pl.pallas_call(
-            forward_kernel,
-            grid=(modes,),
-            out_shape=(
-                jax.ShapeDtypeStruct((modes, 2, size, size), F32),
-                jax.ShapeDtypeStruct((size, size), F32),
-            ),
-            in_specs=[mode_spec, whole(2, size, size), table_spec, table_spec],
-            out_specs=(mode_spec, whole(size, size)),
-            scratch_shapes=buffers,
-            compiler_params=PARAMS,
-        )(probe, patch, forward, inverse)
-        power = power + swap(power) if groups == 2 else lax.psum(power, "mode")
-        term, grad = pl.pallas_call(
-            backward_kernel,
-            grid=(modes,),
-            out_shape=(jax.ShapeDtypeStruct((modes, 2, size, size), BF16), wave_shape),
-            in_specs=[
-                mode_spec,
-                mode_spec,
-                whole(2, size, size),
-                whole(size, size),
-                whole(size, size),
-                table_spec,
-                table_spec,
-            ],
-            out_specs=(mode_spec, whole(2, size, size)),
-            scratch_shapes=[pltpu.VMEM((size, size), F32)] + buffers,
-            compiler_params=PARAMS,
-        )(far, probe, patch, amplitude[0], power, inverse, forward)
-        probe_grad = lax.psum(term, "scan").astype(F32)
+        )(strips, pos_row, all_cols, probe, patch, amplitude[0], forward, inverse)
+        return (strip_grad, term.astype(F32))
+
+    far, power = pl.pallas_call(
+        forward_kernel,
+        grid=(modes,),
+        out_shape=(
+            jax.ShapeDtypeStruct((modes, 2, size, size), F32),
+            jax.ShapeDtypeStruct((size, size), F32),
+        ),
+        in_specs=[mode_spec, whole(2, size, size), table_spec, table_spec],
+        out_specs=(mode_spec, whole(size, size)),
+        scratch_shapes=buffers,
+        compiler_params=PARAMS,
+    )(probe, patch, forward, inverse)
+    power = power + swap(power) if groups == 2 else lax.psum(power, "mode")
+    term, grad = pl.pallas_call(
+        backward_kernel,
+        grid=(modes,),
+        out_shape=(jax.ShapeDtypeStruct((modes, 2, size, size), BF16), wave_shape),
+        in_specs=[
+            mode_spec,
+            mode_spec,
+            whole(2, size, size),
+            whole(size, size),
+            whole(size, size),
+            table_spec,
+            table_spec,
+        ],
+        out_specs=(mode_spec, whole(2, size, size)),
+        scratch_shapes=[pltpu.VMEM((size, size), F32)] + buffers,
+        compiler_params=PARAMS,
+    )(far, probe, patch, amplitude[0], power, inverse, forward)
+    probe_grad = lax.psum(term, "scan").astype(F32)
 
     if groups == 2:
         mine = lax.dynamic_index_in_dim(grad, me, 0, keepdims=True)

time: 206 us -> 180 us (0.87)
  blocking collectives: 25.4 us -> 0 us
  Pallas kernels: 159 us -> 167 us
  other arithmetic: 14.4 us -> 9.79 us
  waiting for transfers between devices: 2.65 us -> 0 us
    all_to_all x1 -> x0, blocking collectives: 25.4 us -> none  [shards(): lax.all_to_all(pieces.astype(BF16), 'scan', 0, 0, tiled=False).astype(F32)]
    pallas_call x1, Pallas kernels: 114 us -> 128 us  [shards(): pl.pallas_call(core_kernel, out_shape=(jax.ShapeDtypeStruct((modes, 2, si...]
    pallas_call x2 -> x0, Pallas kernels: 6.9 us -> none  [the longest x1 3.86 us: shards(): pl.pallas_call(add_kernel, out_shape=jax.ShapeDtypeStruct((parts, rows, c...]
    ppermute x2 -> x0, waiting for transfers between devices: 2.65 us -> none  [swap(): return lax.ppermute(x, 'mode', [(0, 1), (1, 0)])]
    convert_element_type x3 -> x1, other arithmetic: 9.41 us -> 6.8 us  [shards(): return (strip_grad, term.astype(F32))]
  transfers between devices with their start and end apart: 2 -> 0, of which waited for: 1 -> 0; matrix products, arithmetic and copies ran while one was open for 3% -> 0% of each run, Pallas kernels for 0% -> 0%
where the time goes in v2:
time: 180 us
  Pallas kernels  167 us (93%)
  other arithmetic  9.79 us (5%)
  between operations  2.65 us (1%)
    pallas_call x1, Pallas kernels, shards(): pl.pallas_call(core_kernel, out_shape=(jax.ShapeDtypeStruct((modes, 2, si...  128 us
    pallas_call x1, Pallas kernels, shards(): pl.pallas_call(gather_kernel, out_shape=jax.ShapeDtypeStruct((2, devices,...  32.3 us
    convert_element_type x1, other arithmetic, shards(): return (strip_grad, term.astype(F32))  6.8 us
    pallas_call x1, Pallas kernels, shards(): pl.pallas_call(cut_kernel, out_shape=wave_shape, in_specs=[SMEM, SMEM, SM...  5.99 us

profile of v2, /device:TPU:0, one launch (start us, length us, event | category | flops | bytes accessed | tf_op | source)
XLA Modules:
  0.0 179.8 jit_solution(11189585661968710955)
XLA Ops:
  2.6 1.0 convert_element_type.15
  3.7 0.7 fusion.1.mine
  4.3 32.3 %shard_map.95.held = bf16[2,16,48,1152]{3,2,1,0:T(8,128)(2,1)} custom-call(bf16[48,1152]{1,0:T(8,128)(2,1)} %fusion.1.mine), custom_call_target="tpu_custom_call" | custom-call | tf_op jit(solution)/shard_map/pallas_call | solution.py:541
  36.6 0.8 slice_convert_fusion
  37.4 0.1 copy.11
  37.5 0.5 add_bitcast_fusion
  38.0 6.0 %shard_map.96.patch_hbm = f32[2,512,512]{2,1,0:T(8,128)} custom-call(s32[16]{0:T(128)} %get-tuple-element.7.strips, s32[1]{0:T(128)S(6)} %copy.13.row, s32[1]{0:T(128)} %copy.14.col, bf16[2,16,48,1152]{3,2,1,0:T(8,128)(2,1)} %shard_map.95.held), custom_call_target="tpu_custom_call" | custom-call | tf_op jit(solution)/shard_map/pallas_call | solution.py:565
  44.0 128.3 %shard_map.97 = (bf16[4,2,512,512]{3,2,1,0:T(8,128)(2,1)}, f32[2,40,1152]{2,1,0:T(8,128)}) custom-call(s32[16]{0:T(128)} %get-tuple-element.7.strips, s32[1]{0:T(128)S(6)} %copy.13.row, s32[16]{0:T(128)} %get-tuple-element.6.cols, f32[4,2,512,512]{3,2,1,0:T(8,128)} %probe_hbm.1, f32[2,512,512]{2,1,0:T(8,128)} %shard_map.96.patch_hbm, f32[512,512]{1,0:T(8,128)} %bitcast.15, ...), custom_call_target="tpu_custom_call" | custom-call | tf_op jit(solution)/shard_map/pallas_call | solution.py:587
  172.3 0.0 copy-start
  172.3 6.8 %convert_element_type.19 = f32[4,2,512,512]{3,2,1,0:T(8,128)} convert(bf16[4,2,512,512]{3,2,1,0:T(8,128)(2,1)} %get-tuple-element.5) | non-fusion elementwise | flops 2097152 | bytes 12582912 | tf_op jit(solution)/shard_map/convert_element_type | solution.py:639
  179.1 0.0 copy-done
  179.1 0.7 copy.16
  (3 shorter events, 0.0 us)
Async XLA Ops:
  172.3 6.8 %copy-start = (f32[2,40,1152]{2,1,0:T(8,128)S(1)}, f32[2,40,1152]{2,1,0:T(8,128)}, u32[]{:S(2)}) copy-start(f32[2,40,1152]{2,1,0:T(8,128)} %get-tuple-element.10) | copy-start | bytes 1105924

commit v3 on v2

--- a/solution.py
+++ b/solution.py
@@ -354,8 +354,6 @@
             return carry
 
         lax.fori_loop(0, devices * deep // TILE, move, 0)
-        for k in range(1, devices):
-            piece(k).start()
         landed[mine] = pieces[mine]
 
     def add_pieces():
@@ -469,6 +467,9 @@
         finish(s, m)
         if s < 6:
             start(s + 1, m)
+        if s == 3:
+            for k in range(1 + m, devices, modes):
+                piece(k).start()
 
     def drain(m, carry):
         for c in range(2):

time: 180 us -> 187 us (1.039)
  Pallas kernels: 167 us -> 173 us
    pallas_call x1, Pallas kernels: 128 us -> 135 us  [shards(): pl.pallas_call(core_kernel, out_shape=(jax.ShapeDtypeStruct((modes, 2, si...]
where the time goes in v3:
time: 187 us; the launch traced here: 186 us
  Pallas kernels  173 us (93%)
  other arithmetic  9.79 us (5%)
  between operations  2.65 us (1%)
    pallas_call x1, Pallas kernels, shards(): pl.pallas_call(core_kernel, out_shape=(jax.ShapeDtypeStruct((modes, 2, si...  135 us
    pallas_call x1, Pallas kernels, shards(): pl.pallas_call(gather_kernel, out_shape=jax.ShapeDtypeStruct((2, devices,...  32.3 us
    convert_element_type x1, other arithmetic, shards(): return (strip_grad, term.astype(F32))  6.8 us
    pallas_call x1, Pallas kernels, shards(): pl.pallas_call(cut_kernel, out_shape=wave_shape, in_specs=[SMEM, SMEM, SM...  5.99 us

profile of v3, /device:TPU:0, one launch (start us, length us, event | category | flops | bytes accessed | tf_op | source)
XLA Modules:
  0.0 186.3 jit_solution(1432491460709824272)
XLA Ops:
  2.6 1.0 convert_element_type.15
  3.7 0.7 fusion.1.mine
  4.3 32.3 %shard_map.95.held = bf16[2,16,48,1152]{3,2,1,0:T(8,128)(2,1)} custom-call(bf16[48,1152]{1,0:T(8,128)(2,1)} %fusion.1.mine), custom_call_target="tpu_custom_call" | custom-call | tf_op jit(solution)/shard_map/pallas_call | solution.py:542
  36.6 0.8 slice_convert_fusion
  37.4 0.1 copy.11
  37.5 0.5 add_bitcast_fusion
  38.0 6.0 %shard_map.96.patch_hbm = f32[2,512,512]{2,1,0:T(8,128)} custom-call(s32[16]{0:T(128)} %get-tuple-element.7.strips, s32[1]{0:T(128)S(6)} %copy.13.row, s32[1]{0:T(128)} %copy.14.col, bf16[2,16,48,1152]{3,2,1,0:T(8,128)(2,1)} %shard_map.95.held), custom_call_target="tpu_custom_call" | custom-call | tf_op jit(solution)/shard_map/pallas_call | solution.py:566
  44.0 134.7 %shard_map.97 = (bf16[4,2,512,512]{3,2,1,0:T(8,128)(2,1)}, f32[2,40,1152]{2,1,0:T(8,128)}) custom-call(s32[16]{0:T(128)} %get-tuple-element.7.strips, s32[1]{0:T(128)S(6)} %copy.13.row, s32[16]{0:T(128)} %get-tuple-element.6.cols, f32[4,2,512,512]{3,2,1,0:T(8,128)} %probe_hbm.1, f32[2,512,512]{2,1,0:T(8,128)} %shard_map.96.patch_hbm, f32[512,512]{1,0:T(8,128)} %bitcast.15, ...), custom_call_target="tpu_custom_call" | custom-call | tf_op jit(solution)/shard_map/pallas_call | solution.py:588
  178.7 0.0 copy-start
  178.7 6.8 %convert_element_type.19 = f32[4,2,512,512]{3,2,1,0:T(8,128)} convert(bf16[4,2,512,512]{3,2,1,0:T(8,128)(2,1)} %get-tuple-element.5) | non-fusion elementwise | flops 2097152 | bytes 12582912 | tf_op jit(solution)/shard_map/convert_element_type | solution.py:640
  185.5 0.0 copy-done
  185.5 0.7 copy.16
  (3 shorter events, 0.0 us)
Async XLA Ops:
  178.7 6.8 %copy-start = (f32[2,40,1152]{2,1,0:T(8,128)S(1)}, f32[2,40,1152]{2,1,0:T(8,128)}, u32[]{:S(2)}) copy-start(f32[2,40,1152]{2,1,0:T(8,128)} %get-tuple-element.10) | copy-start | bytes 1105924

commit v4 on v2

--- a/solution.py
+++ b/solution.py
@@ -189,12 +189,12 @@
 
 
 def core_kernel(
-    strips, row, cols, probe_hbm, patch_hbm, measured_hbm, left_hbm, right_hbm, result, strip_grad,
-    probe, patch, measured, left, right,
+    strip_of, row, col, field, probe_hbm, measured_hbm, left_hbm, right_hbm, result, strip_grad,
+    metas, held_a, held_b, col_hot, row_hot, cut, probe, patch, measured, left, right,
     far, power, power_in, scale, wave, half, term, got1, sum1, got2, sum2, got3,
     grad, grad_in, summed, pieces, landed,
-    load, load_probe, swap_send, swap_recv, send, recv, send_z, recv_z, ship_z, land_z,
-    part_send, part_recv, piece_send, piece_recv, strip_send, strip_recv,
+    load, load_probe, meta_send, meta_recv, hop_send, hop_recv, swap_send, swap_recv, send, recv,
+    send_z, recv_z, ship_z, land_z, part_send, part_recv, piece_send, piece_recv, strip_send, strip_recv,
 ):
     modes, size = probe.shape[0], patch.shape[-1]
     devices = lax.axis_size("scan")
@@ -209,6 +209,7 @@
     first_peer, second_peer = (peer_x, peer_y), (peer_y, peer_x)
     first_at, second_at = (x, y), (y, x)
     h, q, e = size // 2, size // 4, size // 4 // planes
+    deep = pieces.shape[0] // devices
 
     barrier = pltpu.get_barrier_semaphore()
     everyone = [partner] + [(lax.rem(scan + k, devices), mode) for k in range(1, devices)]
@@ -218,15 +219,35 @@
     def probe_load(m):
         return pltpu.make_async_copy(probe_hbm.at[m], probe.at[m], load_probe.at[m])
 
-    whole = [(patch_hbm, patch), (left_hbm, left), (right_hbm, right), (measured_hbm, measured)]
+    whole = [(left_hbm, left), (right_hbm, right), (measured_hbm, measured)]
     loads = [pltpu.make_async_copy(src, dst, load.at[i]) for i, (src, dst) in enumerate(whole)]
     probe_load(0).start()
     for copy in loads:
         copy.start()
     for m in range(1, modes):
         probe_load(m).start()
-    for copy in loads:
-        copy.wait()
+
+    def rows(start, count, step):
+        return pl.ds(pl.multiple_of(start, step), count)
+
+    def one_hot(mask):
+        return jnp.where(mask, 1.0, 0.0).astype(BF16)
+
+    held, parts_at = (held_a, held_b), (0, held_a.shape[1], width)
+    plane, plane_x, plane_y = y * 2 + x, y * 2 + 1 - x, (1 - y) * 2 + x
+    plane_d = (1 - y) * 2 + 1 - x
+
+    levels = (z, z + 1 - 2 * lax.rem(z, 2), z + 2 - 4 * (z // 2), 3 - z)
+
+    def strip_rows(side, k):
+        return rows((side * planes + levels[k]) * deep, deep, deep)
+
+    own = jnp.concatenate([field[mode].astype(BF16), jnp.zeros((deep - strip, width), BF16)])
+    for i in range(2):
+        held[i][strip_rows(plane, 0)] = own[:, parts_at[i] : parts_at[i + 1]]
+    which = lax.broadcasted_iota(jnp.int32, (8, LANES), 0)
+    numbers = jnp.where(which == 1, lax.rem(col[0], LANES), col[0] // LANES)
+    metas[scan] = jnp.where(which == 0, strip_of[0], numbers)
     pl.semaphore_wait(barrier, len(everyone))
 
     def remote(src, dst, send_sem, recv_sem, peer):
@@ -234,8 +255,101 @@
             src_ref=src, dst_ref=dst, send_sem=send_sem, recv_sem=recv_sem, device_id=peer, device_id_type=MESH
         )
 
-    def rows(start, count, step):
-        return pl.ds(pl.multiple_of(start, step), count)
+    def meta(k, back=0):
+        at = lax.rem(scan + devices - back, devices)
+        to = (lax.rem(scan + k, devices), mode)
+        return remote(metas.at[at], metas.at[at], meta_send.at[k - 1], meta_recv.at[k - 1], to)
+
+    def hop(kind, i, k, side, peer):
+        at = held[i].at[strip_rows(side, k)]
+        return remote(at, at, hop_send.at[kind, i, k], hop_recv.at[kind, i, k], peer)
+
+    def hop_z(i, k):
+        at = held[i].at[strip_rows(plane, 0)]
+        return remote(at, at, hop_send.at[0, i, k], hop_recv.at[0, i, k], (levels[k] * 4 + plane, mode))
+
+    def spread(k):
+        for i in range(2):
+            hop(1, i, k, plane, peer_x).start()
+            hop(2, 1 - i, k, plane, peer_y).start()
+
+    def relay(k):
+        hop(1, 0, k, plane_x, peer_x).wait_recv()
+        hop(3, 0, k, plane_x, peer_y).start()
+        hop(2, 1, k, plane_y, peer_y).wait_recv()
+        hop(3, 1, k, plane_y, peer_x).start()
+
+    def cut_columns(side):
+        at = rows(side * planes * deep, planes * deep, planes * deep)
+        got = jnp.dot(held_a[at], col_hot[: held_a.shape[1]], preferred_element_type=F32)
+        got = got + jnp.dot(held_b[at], col_hot[held_a.shape[1] :], preferred_element_type=F32)
+        cut[at] = got.astype(BF16)
+
+    def patch_swap(i):
+        at = rows(i * TILE, TILE, TILE)
+        own = patch.at[mode, at]
+        return remote(own, own, hop_send.at[4, i, 0], hop_recv.at[4, i, 0], partner)
+
+    def across_lanes(row_values, count):
+        return jnp.concatenate([row_values] * (count // LANES), axis=1)
+
+    for k in range(1, devices):
+        meta(k).start()
+    for k in range(1, planes):
+        hop_z(0, k).start()
+        hop_z(1, k).start()
+    spread(0)
+
+    def column_hot(i, carry):
+        at = rows(i * LANES, LANES, LANES)
+        lane = lax.broadcasted_iota(jnp.int32, (LANES, size), 1)
+        col_hot[at] = one_hot(lax.broadcasted_iota(jnp.int32, (LANES, size), 0) + i * LANES - lane == col[0])
+        return carry
+
+    lax.fori_loop(0, width // LANES, column_hot, 0)
+    for k in range(1, planes):
+        hop(0, 0, k, plane, partner).wait_recv()
+        hop(0, 1, k, plane, partner).wait_recv()
+        spread(k)
+        relay(k - 1)
+    cut_columns(plane)
+    relay(planes - 1)
+    for k in range(1, devices):
+        meta(k, k).wait_recv()
+    lane = lax.broadcasted_iota(jnp.int32, (8, devices * deep), 1)
+    target = jnp.full((8, devices * deep), -1, jnp.int32)
+    for j in range(devices):
+        ahead = lane - (j % 4 * planes + j // 4) * deep
+        target = jnp.where(
+            (ahead >= 0) & (ahead < strip), across_lanes(metas[j, :1], devices * deep) * strip + ahead, target
+        )
+    target = target[:1] - row[0]
+
+    def line_hot(i, carry):
+        at = rows(i * 64, 64, 64)
+        line = lax.broadcasted_iota(jnp.int32, (64, devices * deep), 0) + i * 64
+        row_hot[at] = one_hot(line == target)
+        return carry
+
+    lax.fori_loop(0, size // 64, line_hot, 0)
+    for k in range(planes):
+        hop(1, 1, k, plane_x, peer_x).wait_recv()
+    cut_columns(plane_x)
+    for k in range(planes):
+        hop(2, 0, k, plane_y, peer_y).wait_recv()
+    cut_columns(plane_y)
+    for k in range(planes):
+        hop(3, 0, k, plane_d, peer_y).wait_recv()
+        hop(3, 1, k, plane_d, peer_x).wait_recv()
+    cut_columns(plane_d)
+    for i in range(size // TILE):
+        at = pl.ds(i * TILE, TILE)
+        patch[mode, at] = jnp.dot(row_hot[at], cut[...], preferred_element_type=F32).astype(BF16)
+        patch_swap(i).start()
+    for copy in loads:
+        copy.wait()
+    for i in range(size // TILE):
+        patch_swap(i).wait_recv()
 
     def copy1(m, c):
         away = rows((1 - first_at[c]) * h, h, h)
@@ -317,11 +431,7 @@
         at = rows(i * TILE, TILE, TILE)
         return remote(grad.at[1 - mode, at], grad_in.at[at], part_send.at[i], part_recv.at[i], partner)
 
-    deep = pieces.shape[0] // devices
     mine = rows(scan * deep, deep, deep)
-
-    def one_hot(mask):
-        return jnp.where(mask, 1.0, 0.0).astype(BF16)
 
     def piece(k):
         to = lax.rem(scan + k, devices)
@@ -343,7 +453,8 @@
         ahead = lax.broadcasted_iota(jnp.int32, (deep, size), 1) - lax.broadcasted_iota(jnp.int32, (deep, size), 0)
 
         def pick(j, carry):
-            wave[rows(j * deep, deep, deep)] = one_hot(ahead == strips[j] * strip - row[0])
+            begin = across_lanes(metas[j, :1], size) * strip - row[0]
+            wave[rows(j * deep, deep, deep)] = one_hot(ahead == begin)
             return carry
 
         lax.fori_loop(0, devices, pick, 0)
@@ -367,7 +478,7 @@
         ahead = ahead - lax.broadcasted_iota(jnp.int32, (LANES, 2 * LANES), 0)
 
         def one(j, carry):
-            turn = one_hot(ahead == lax.rem(cols[j], LANES))
+            turn = one_hot(ahead == across_lanes(metas[j, 1:2], 2 * LANES))
             blocks = jnp.concatenate(
                 [landed[rows(j * deep, deep, deep), b * LANES : (b + 1) * LANES] for b in range(parts)]
             )
@@ -379,7 +490,7 @@
                 for t in range((width - size) // LANES + 1):
                     if b + t < width // LANES:
                         to = slice((b + t) * LANES, (b + t + 1) * LANES)
-                        strip_grad[mode, :, to] += jnp.where(cols[j] // LANES == t, here, 0.0)
+                        strip_grad[mode, :, to] += jnp.where(metas[j, 2:3] == t, here, 0.0)
             return carry
 
         lax.fori_loop(0, devices, one, 0)
@@ -390,7 +501,7 @@
 
         def leave(i, carry):
             at, low = rows(i * 64, 64, 64), rows(size + i * 64, 64, 64)
-            pr, pi, xr, xi = probe[m, 0, at], probe[m, 1, at], patch[0, at], patch[1, at]
+            pr, pi, xr, xi = probe[m, 0, at], probe[m, 1, at], patch[0, at].astype(F32), patch[1, at].astype(F32)
             wave[at] = (pr * xr - pi * xi).astype(BF16)
             wave[low] = (pr * xi + pi * xr).astype(BF16)
             return carry
@@ -437,7 +548,7 @@
             at = rows(i * TILE, TILE, TILE)
             both = jnp.dot(half[at], left[...], preferred_element_type=F32)
             br, bi = both[:, :size], both[:, size:]
-            pr, pi, xr, xi = probe[m, 0, at], probe[m, 1, at], patch[0, at], patch[1, at]
+            pr, pi, xr, xi = probe[m, 0, at], probe[m, 1, at], patch[0, at].astype(F32), patch[1, at].astype(F32)
             term[m, 0, at] = (xr * br + xi * bi).astype(BF16)
             term[m, 1, at] = (xr * bi - xi * br).astype(BF16)
             re, im = pr * br + pi * bi, pr * bi - pi * br
@@ -486,6 +597,17 @@
     for k in range(1, devices):
         piece(k).wait_send()
     strip_swap().wait()
+    for i in range(size // TILE):
+        patch_swap(i).wait_send()
+    for k in range(1, devices):
+        meta(k).wait_send()
+    for i in range(2):
+        for k in range(planes):
+            if k:
+                hop_z(i, k).wait_send()
+            hop(1, i, k, plane, peer_x).wait_send()
+            hop(2, i, k, plane, peer_y).wait_send()
+            hop(3, i, k, (plane_x, plane_y)[i], (peer_y, peer_x)[i]).wait_send()
 
 
 def place_kernel(strips, row, grad, out, padded):
@@ -531,6 +653,78 @@
 
     def swap(x):
         return lax.ppermute(x, "mode", [(0, 1), (1, 0)])
+
+    planes, deep = devices // 4, -(-rows // 16) * 16
+    fits = groups == 2 and devices == 4 * planes and planes == 4 and size % (64 * planes) == 0
+    fits = fits and cols % LANES == 0 and size // TILE == 2
+    if fits and rows % 8 == 0 and devices * deep % TILE == 0 and devices * deep <= 2 * size:
+        dma = pltpu.SemaphoreType.DMA
+        h, q, e = size // 2, size // 4, size // 4 // planes
+        vmem, lanes = pltpu.VMEM, (cols // LANES + 1) // 2 * LANES
+        any_space = pl.BlockSpec(memory_space=pl.ANY)
+        term, strip_grad = pl.pallas_call(
+            core_kernel,
+            out_shape=(
+                jax.ShapeDtypeStruct((modes, 2, size, size), BF16),
+                jax.ShapeDtypeStruct((2, rows, cols), F32),
+            ),
+            in_specs=[SMEM] * 3 + [VMEM] + [any_space] * 4,
+            out_specs=(VMEM, VMEM),
+            scratch_shapes=[
+                vmem((devices, 8, LANES), jnp.int32),
+                vmem((devices * deep, lanes), BF16),
+                vmem((devices * deep, cols - lanes), BF16),
+                vmem((cols, size), BF16),
+                vmem((size, devices * deep), BF16),
+                vmem((devices * deep, size), BF16),
+                vmem((modes, 2, size, size), F32),
+                vmem((2, size, size), BF16),
+                vmem((size, size), F32),
+                vmem((2 * size, 2 * size), BF16),
+                vmem((2 * size, 2 * size), BF16),
+                vmem((modes, 2, size, size), F32),
+                vmem((size, size), F32),
+                vmem((size, size), F32),
+                vmem((size, size), F32),
+                vmem((2 * size, size), BF16),
+                vmem((size, 2 * size), BF16),
+                vmem((modes, 2, size, size), BF16),
+                vmem((modes, 2, h, size), BF16),
+                vmem((modes, 2, h, size), BF16),
+                vmem((modes, 2, q, size), BF16),
+                vmem((modes, 2, q, size), BF16),
+                vmem((modes, 2, planes - 1, e, size), BF16),
+                vmem((2, size, size), F32),
+                vmem((size, size), F32),
+                vmem((size, size), BF16),
+                vmem((devices * deep, size), BF16),
+                vmem((devices * deep, size), BF16),
+                dma((3,)),
+                dma((modes,)),
+                dma((devices - 1,)),
+                dma((devices - 1,)),
+                dma((5, 2, planes)),
+                dma((5, 2, planes)),
+                dma((size // TILE,)),
+                dma((size // TILE,)),
+                dma((4, modes, 2)),
+                dma((4, modes, 2)),
+                dma((modes, 2, planes - 1)),
+                dma((modes, 2, planes - 1)),
+                dma((modes, 2, planes - 1)),
+                dma((modes, 2, planes - 1)),
+                dma((size // TILE,)),
+                dma((size // TILE,)),
+                dma((devices - 1,)),
+                dma((devices - 1,)),
+                dma,
+                dma,
+            ],
+            compiler_params=pltpu.CompilerParams(
+                vmem_limit_bytes=60 * 1024 * 1024, collective_id=0, has_side_effects=True
+            ),
+        )(strip_of, pos_row, pos_col, object_field, probe, amplitude[0], forward, inverse)
+        return (strip_grad, term.astype(F32))
 
     lane = lax.broadcasted_iota(jnp.int32, (2, META, cols), 2)
     numbers = jnp.where(lane == 0, strip_of[0], jnp.where(lane == 1, pos_col[0] // LANES, pos_col[0] % LANES))
@@ -577,67 +771,6 @@
     mode_spec = pl.BlockSpec((1, 2, size, size), lambda m: (m, 0, 0, 0))
     table_spec = whole(2 * size, 2 * size)
     buffers = [pltpu.VMEM((2 * size, size), BF16), pltpu.VMEM((size, 2 * size), BF16)]
-    planes, deep = devices // 4, -(-rows // 16) * 16
-    fits = groups == 2 and devices == 4 * planes and planes >= 2 and size % (64 * planes) == 0
-    if fits and rows % 8 == 0 and devices * deep % TILE == 0 and devices * deep <= 2 * size:
-        dma = pltpu.SemaphoreType.DMA
-        h, q, e = size // 2, size // 4, size // 4 // planes
-        vmem = pltpu.VMEM
-        any_space = pl.BlockSpec(memory_space=pl.ANY)
-        term, strip_grad = pl.pallas_call(
-            core_kernel,
-            out_shape=(
-                jax.ShapeDtypeStruct((modes, 2, size, size), BF16),
-                jax.ShapeDtypeStruct((2, rows, cols), F32),
-            ),
-            in_specs=[SMEM] * 3 + [any_space] * 5,
-            out_specs=(VMEM, VMEM),
-            scratch_shapes=[
-                vmem((modes, 2, size, size), F32),
-                vmem((2, size, size), F32),
-                vmem((size, size), F32),
-                vmem((2 * size, 2 * size), BF16),
-                vmem((2 * size, 2 * size), BF16),
-                vmem((modes, 2, size, size), F32),
-                vmem((size, size), F32),
-                vmem((size, size), F32),
-                vmem((size, size), F32),
-                vmem((2 * size, size), BF16),
-                vmem((size, 2 * size), BF16),
-                vmem((modes, 2, size, size), BF16),
-                vmem((modes, 2, h, size), BF16),
-                vmem((modes, 2, h, size), BF16),
-                vmem((modes, 2, q, size), BF16),
-                vmem((modes, 2, q, size), BF16),
-                vmem((modes, 2, planes - 1, e, size), BF16),
-                vmem((2, size, size), F32),
-                vmem((size, size), F32),
-                vmem((size, size), BF16),
-                vmem((devices * deep, size), BF16),
-                vmem((devices * deep, size), BF16),
-                dma((4,)),
-                dma((modes,)),
-                dma((size // TILE,)),
-                dma((size // TILE,)),
-                dma((4, modes, 2)),
-                dma((4, modes, 2)),
-                dma((modes, 2, planes - 1)),
-                dma((modes, 2, planes - 1)),
-                dma((modes, 2, planes - 1)),
-                dma((modes, 2, planes - 1)),
-                dma((size // TILE,)),
-                dma((size // TILE,)),
-                dma((devices - 1,)),
-                dma((devices - 1,)),
-                dma,
-                dma,
-            ],
-            compiler_params=pltpu.CompilerParams(
-                vmem_limit_bytes=58 * 1024 * 1024, collective_id=1, has_side_effects=True
-            ),
-        )(strips, pos_row, all_cols, probe, patch, amplitude[0], forward, inverse)
-        return (strip_grad, term.astype(F32))
-
     far, power = pl.pallas_call(
         forward_kernel,
         grid=(modes,),

time: 180 us -> 164 us (0.911)
  Pallas kernels: 167 us -> 153 us
  other arithmetic: 9.79 us -> 6.8 us
    pallas_call x2 -> x0, Pallas kernels: 38.3 us -> none  [the longest x1 32.3 us: shards(): pl.pallas_call(gather_kernel, out_shape=jax.ShapeDtypeStruct((2, devices,...]
    pallas_call x1, Pallas kernels: 128 us -> 153 us  [shards(): pl.pallas_call(core_kernel, out_shape=(jax.ShapeDtypeStruct((modes, 2, si...]
where the time goes in v4:
time: 164 us; the launch traced here: 163 us
  Pallas kernels  153 us (93%)
  other arithmetic  6.8 us (4%)
  between operations  2.58 us (2%)
    pallas_call x1, Pallas kernels, shards(): pl.pallas_call(core_kernel, out_shape=(jax.ShapeDtypeStruct((modes, 2, si...  153 us
    convert_element_type x1, other arithmetic, shards(): return (strip_grad, term.astype(F32))  6.8 us

profile of v4, /device:TPU:0, one launch (start us, length us, event | category | flops | bytes accessed | tf_op | source)
XLA Modules:
  0.0 163.3 jit_solution(6598167144750352379)
XLA Ops:
  2.6 153.2 %shard_map.95 = (bf16[4,2,512,512]{3,2,1,0:T(8,128)(2,1)}, f32[2,40,1152]{2,1,0:T(8,128)}) custom-call(s32[1]{0:T(128)S(6)} %copy.13.strip_of, s32[1]{0:T(128)S(6)} %copy.11.row, s32[1]{0:T(128)S(6)} %copy.12.col, f32[2,40,1152]{2,1,0:T(8,128)} %field.1, f32[4,2,512,512]{3,2,1,0:T(8,128)} %probe_hbm.1, f32[512,512]{1,0:T(8,128)} %bitcast.1, ...), custom_call_target="tpu_custom_call" | custom-call | tf_op jit(solution)/shard_map/pallas_call | solution.py:665
  155.8 0.0 copy-start
  155.8 6.8 %convert_element_type.3 = f32[4,2,512,512]{3,2,1,0:T(8,128)} convert(bf16[4,2,512,512]{3,2,1,0:T(8,128)(2,1)} %get-tuple-element.5) | non-fusion elementwise | flops 2097152 | bytes 12582912 | tf_op jit(solution)/shard_map/convert_element_type | solution.py:727
  162.6 0.0 copy-done
  162.6 0.7 copy.14
Async XLA Ops:
  155.8 6.8 %copy-start = (f32[2,40,1152]{2,1,0:T(8,128)S(1)}, f32[2,40,1152]{2,1,0:T(8,128)}, u32[]{:S(2)}) copy-start(f32[2,40,1152]{2,1,0:T(8,128)} %get-tuple-element.8) | copy-start | bytes 1105924

commit v5 on v4

--- a/solution.py
+++ b/solution.py
@@ -11,9 +11,18 @@
 F32 = jnp.float32
 BF16 = jnp.bfloat16
 LANES = 128
+HALVES = 2
 META = 8
 PLANE = 4
 TILE = 256
+ORDER = (
+    (0, 0), (0, 1), (0, 2), (1, 0), (1, 1), (0, 3), (0, 4), (2, 0), (2, 1), (1, 2),
+    (1, 3), (0, 5), (3, 0), (1, 4), (2, 2), (3, 1), (0, 6), (4, 0), (3, 2), (4, 1),
+    (2, 4), (1, 6), (4, 2), (1, 5), (2, 3), (0, 7), (5, 2), (3, 4), (3, 3), (1, 7),
+    (2, 6), (4, 4), (4, 3), (5, 1), (2, 5), (7, 0), (5, 4), (5, 3), (2, 7), (3, 6),
+    (3, 7), (3, 5), (5, 0), (4, 6), (8, 0), (5, 6), (4, 5), (4, 7), (8, 1), (8, 2),
+    (5, 5), (5, 7), (9, 0),
+)
 PARAMS = pltpu.CompilerParams(vmem_limit_bytes=56 * 1024 * 1024)
 VMEM = pl.BlockSpec(memory_space=pltpu.VMEM)
 SMEM = pl.BlockSpec(memory_space=pltpu.SMEM)
@@ -208,7 +217,8 @@
     peers_z = [mesh_peer(scan, mode, planes, 0, 0, k) for k in range(1, planes)]
     first_peer, second_peer = (peer_x, peer_y), (peer_y, peer_x)
     first_at, second_at = (x, y), (y, x)
-    h, q, e = size // 2, size // 4, size // 4 // planes
+    chunk = size // HALVES
+    h, q, e = chunk // 2, chunk // 4, chunk // 4 // planes
     deep = pieces.shape[0] // devices
 
     barrier = pltpu.get_barrier_semaphore()
@@ -351,81 +361,81 @@
     for i in range(size // TILE):
         patch_swap(i).wait_recv()
 
-    def copy1(m, c):
-        away = rows((1 - first_at[c]) * h, h, h)
-        return remote(term.at[m, c, away], got1.at[m, c], send.at[0, m, c], recv.at[0, m, c], first_peer[c])
-
-    def copy2(m, c):
+    def place(u):
+        return u // HALVES, u % HALVES * chunk
+
+    def copy1(u, c):
+        m, low = place(u)
+        away = rows(low + (1 - first_at[c]) * h, h, h)
+        return remote(term.at[m, c, away], got1.at[u, c], send.at[0, u, c], recv.at[0, u, c], first_peer[c])
+
+    def copy2(u, c):
         away = rows((1 - second_at[c]) * q, q, q)
-        return remote(sum1.at[m, c, away], got2.at[m, c], send.at[1, m, c], recv.at[1, m, c], second_peer[c])
-
-    def copy3(m, c, k):
+        return remote(sum1.at[u, c, away], got2.at[u, c], send.at[1, u, c], recv.at[1, u, c], second_peer[c])
+
+    def copy3(u, c, k):
         away = rows(lax.rem(z + k, planes) * e, e, e)
         return remote(
-            sum2.at[m, c, away], got3.at[m, c, k - 1], send_z.at[m, c, k - 1], recv_z.at[m, c, k - 1], peers_z[k - 1]
+            sum2.at[u, c, away], got3.at[u, c, k - 1], send_z.at[u, c, k - 1], recv_z.at[u, c, k - 1], peers_z[k - 1]
         )
 
-    def base(c):
-        return first_at[c] * h + second_at[c] * q
-
-    def copy4(m, c, k):
-        own = result.at[m, c, rows(base(c) + z * e, e, e)]
-        return remote(own, own, ship_z.at[m, c, k - 1], land_z.at[m, c, k - 1], peers_z[k - 1])
-
-    def copy5(m, c):
-        own = result.at[m, c, rows(base(c), q, q)]
-        return remote(own, own, send.at[2, m, c], recv.at[2, m, c], second_peer[c])
-
-    def copy6(m, c):
-        own = result.at[m, c, rows(first_at[c] * h, h, h)]
-        return remote(own, own, send.at[3, m, c], recv.at[3, m, c], first_peer[c])
-
-    def start(stage, m):
+    def base(u, c):
+        return place(u)[1] + first_at[c] * h + second_at[c] * q
+
+    def copy4(u, c, k):
+        own = result.at[place(u)[0], c, rows(base(u, c) + z * e, e, e)]
+        return remote(own, own, ship_z.at[u, c, k - 1], land_z.at[u, c, k - 1], peers_z[k - 1])
+
+    def copy5(u, c):
+        own = result.at[place(u)[0], c, rows(base(u, c), q, q)]
+        return remote(own, own, send.at[2, u, c], recv.at[2, u, c], second_peer[c])
+
+    def copy6(u, c):
+        m, low = place(u)
+        own = result.at[m, c, rows(low + first_at[c] * h, h, h)]
+        return remote(own, own, send.at[3, u, c], recv.at[3, u, c], first_peer[c])
+
+    def start(stage, u):
         for c in range(2):
             if stage in (3, 4):
                 for k in range(1, planes):
-                    (copy3, copy4)[stage - 3](m, c, k).start()
+                    (copy3, copy4)[stage - 3](u, c, k).start()
             else:
-                {1: copy1, 2: copy2, 5: copy5, 6: copy6}[stage](m, c).start()
-
-    def finish(stage, m):
+                {1: copy1, 2: copy2, 5: copy5, 6: copy6}[stage](u, c).start()
+
+    def finish(stage, u):
+        m, low = place(u)
         for c in range(2):
             if stage == 1:
-                copy1(m, c).wait_recv()
-                mine = term[m, c, rows(first_at[c] * h, h, h)].astype(F32)
-                sum1[m, c] = (mine + got1[m, c].astype(F32)).astype(BF16)
+                copy1(u, c).wait_recv()
+                mine = term[m, c, rows(low + first_at[c] * h, h, h)].astype(F32)
+                sum1[u, c] = (mine + got1[u, c].astype(F32)).astype(BF16)
             if stage == 2:
-                copy2(m, c).wait_recv()
-                mine = sum1[m, c, rows(second_at[c] * q, q, q)].astype(F32)
-                sum2[m, c] = (mine + got2[m, c].astype(F32)).astype(BF16)
+                copy2(u, c).wait_recv()
+                mine = sum1[u, c, rows(second_at[c] * q, q, q)].astype(F32)
+                sum2[u, c] = (mine + got2[u, c].astype(F32)).astype(BF16)
             if stage == 3:
-                total = sum2[m, c, rows(z * e, e, e)].astype(F32)
+                total = sum2[u, c, rows(z * e, e, e)].astype(F32)
                 for k in range(1, planes):
-                    copy3(m, c, k).wait_recv()
-                    total = total + got3[m, c, k - 1].astype(F32)
-                result[m, c, rows(base(c) + z * e, e, e)] = total.astype(BF16)
+                    copy3(u, c, k).wait_recv()
+                    total = total + got3[u, c, k - 1].astype(F32)
+                result[m, c, rows(base(u, c) + z * e, e, e)] = total.astype(BF16)
             if stage == 4:
                 for k in range(1, planes):
-                    copy4(m, c, k).wait_recv()
+                    copy4(u, c, k).wait_recv()
             if stage == 5:
-                copy5(m, c).wait_recv()
+                copy5(u, c).wait_recv()
             if stage == 6:
-                copy6(m, c).wait_recv()
+                copy6(u, c).wait_recv()
 
     def swap(i):
         at = rows(i * TILE, TILE, TILE)
         return remote(power.at[at], power_in.at[at], swap_send.at[i], swap_recv.at[i], partner)
 
     def product(table, source):
-        for c in range(2):
-
-            def down(i, carry, c=c):
-                at = rows(c * size + i * TILE, TILE, TILE)
-                out = jnp.dot(table[at], source[...], preferred_element_type=F32)
-                half[rows(i * TILE, TILE, TILE), c * size : (c + 1) * size] = out.astype(BF16)
-                return carry
-
-            lax.fori_loop(0, size // TILE, down, 0)
+        out = jnp.dot(table[...], source[...], preferred_element_type=F32)
+        half[:, :size] = out[:size].astype(BF16)
+        half[:, size:] = out[size:].astype(BF16)
 
     def part(i):
         at = rows(i * TILE, TILE, TILE)
@@ -465,8 +475,6 @@
             return carry
 
         lax.fori_loop(0, devices * deep // TILE, move, 0)
-        for k in range(1, devices):
-            piece(k).start()
         landed[mine] = pieces[mine]
 
     def add_pieces():
@@ -534,7 +542,7 @@
         total = jnp.maximum(power[at] + power_in[at], 0.25)
         scale[at] = 1.0 - measured[at] / jnp.sqrt(total)
 
-    def backward(m, carry):
+    def backward(m):
         def residual(i, carry):
             at, low = rows(i * 64, 64, 64), rows(size + i * 64, 64, 64)
             wave[at] = (far[m, 0, at] * scale[at]).astype(BF16)
@@ -544,53 +552,47 @@
         lax.fori_loop(0, size // 64, residual, 0)
         product(right, wave)
 
-        def across(i, carry):
-            at = rows(i * TILE, TILE, TILE)
-            both = jnp.dot(half[at], left[...], preferred_element_type=F32)
-            br, bi = both[:, :size], both[:, size:]
-            pr, pi, xr, xi = probe[m, 0, at], probe[m, 1, at], patch[0, at].astype(F32), patch[1, at].astype(F32)
-            term[m, 0, at] = (xr * br + xi * bi).astype(BF16)
-            term[m, 1, at] = (xr * bi - xi * br).astype(BF16)
-            re, im = pr * br + pi * bi, pr * bi - pi * br
-            grad[0, at] = jnp.where(m == 0, re, grad[0, at] + re)
-            grad[1, at] = jnp.where(m == 0, im, grad[1, at] + im)
-
-            @pl.when(m == modes - 1)
-            def _():
-                part(i).start()
-
-            return carry
-
-        lax.fori_loop(0, size // TILE, across, 0)
-        start(1, m)
-
-        @pl.when(m >= 2)
-        def _():
-            finish(1, m - 2)
-            start(2, m - 2)
-
-        return carry
-
-    lax.fori_loop(0, modes, backward, 0)
-    steps = sorted((m + s, -s, m, s) for m in range(modes) for s in range(1, 7) if s > 1 or m >= modes - 2)
-    cut_pieces()
-    for _, _, m, s in steps:
-        if (m, s) == (1, 6):
+    def across_back(m, i):
+        at = pl.ds(i * TILE, TILE)
+        both = jnp.dot(half[at], left[...], preferred_element_type=F32)
+        br, bi = both[:, :size], both[:, size:]
+        pr, pi, xr, xi = probe[m, 0, at], probe[m, 1, at], patch[0, at].astype(F32), patch[1, at].astype(F32)
+        term[m, 0, at] = (xr * br + xi * bi).astype(BF16)
+        term[m, 1, at] = (xr * bi - xi * br).astype(BF16)
+        re, im = pr * br + pi * bi, pr * bi - pi * br
+        grad[0, at] = re if m == 0 else grad[0, at] + re
+        grad[1, at] = im if m == 0 else grad[1, at] + im
+        if m == modes - 1:
+            part(i).start()
+
+    for step, u in ORDER:
+        if step == 0:
+            if u % HALVES == 0:
+                backward(u // HALVES)
+            across_back(u // HALVES, u % HALVES)
+            start(1, u)
+        elif step < 6:
+            finish(step, u)
+            start(step + 1, u)
+        elif step == 7:
+            cut_pieces()
+        elif step == 8:
+            for k in range(1 + u, devices, 3):
+                piece(k).start()
+        else:
             add_pieces()
-        finish(s, m)
-        if s < 6:
-            start(s + 1, m)
-
-    def drain(m, carry):
+
+    def drain(u):
         for c in range(2):
             for copy in (copy1, copy2, copy5, copy6):
-                copy(m, c).wait_send()
+                copy(u, c).wait_send()
             for k in range(1, planes):
-                copy3(m, c, k).wait_send()
-                copy4(m, c, k).wait_send()
-        return carry
-
-    lax.fori_loop(0, modes, drain, 0)
+                copy3(u, c, k).wait_send()
+                copy4(u, c, k).wait_send()
+
+    for u in range(modes * HALVES):
+        finish(6, u)
+        drain(u)
     for i in range(size // TILE):
         swap(i).wait_send()
         part(i).wait_send()
@@ -655,19 +657,17 @@
         return lax.ppermute(x, "mode", [(0, 1), (1, 0)])
 
     planes, deep = devices // 4, -(-rows // 16) * 16
-    fits = groups == 2 and devices == 4 * planes and planes == 4 and size % (64 * planes) == 0
+    fits = groups == 2 and devices == 4 * planes and planes == 4 and size % (64 * HALVES * planes) == 0 and modes * HALVES == 8
     fits = fits and cols % LANES == 0 and size // TILE == 2
     if fits and rows % 8 == 0 and devices * deep % TILE == 0 and devices * deep <= 2 * size:
         dma = pltpu.SemaphoreType.DMA
-        h, q, e = size // 2, size // 4, size // 4 // planes
+        chunks, chunk = modes * HALVES, size // HALVES
+        h, q, e = chunk // 2, chunk // 4, chunk // 4 // planes
         vmem, lanes = pltpu.VMEM, (cols // LANES + 1) // 2 * LANES
         any_space = pl.BlockSpec(memory_space=pl.ANY)
         term, strip_grad = pl.pallas_call(
             core_kernel,
-            out_shape=(
-                jax.ShapeDtypeStruct((modes, 2, size, size), BF16),
-                jax.ShapeDtypeStruct((2, rows, cols), F32),
-            ),
+            out_shape=(vmem((modes, 2, size, size), BF16), vmem((2, rows, cols), F32)),
             in_specs=[SMEM] * 3 + [VMEM] + [any_space] * 4,
             out_specs=(VMEM, VMEM),
             scratch_shapes=[
@@ -689,11 +689,11 @@
                 vmem((2 * size, size), BF16),
                 vmem((size, 2 * size), BF16),
                 vmem((modes, 2, size, size), BF16),
-                vmem((modes, 2, h, size), BF16),
-                vmem((modes, 2, h, size), BF16),
-                vmem((modes, 2, q, size), BF16),
-                vmem((modes, 2, q, size), BF16),
-                vmem((modes, 2, planes - 1, e, size), BF16),
+                vmem((chunks, 2, h, size), BF16),
+                vmem((chunks, 2, h, size), BF16),
+                vmem((chunks, 2, q, size), BF16),
+                vmem((chunks, 2, q, size), BF16),
+                vmem((chunks, 2, planes - 1, e, size), BF16),
                 vmem((2, size, size), F32),
                 vmem((size, size), F32),
                 vmem((size, size), BF16),
@@ -707,12 +707,12 @@
                 dma((5, 2, planes)),
                 dma((size // TILE,)),
                 dma((size // TILE,)),
-                dma((4, modes, 2)),
-                dma((4, modes, 2)),
-                dma((modes, 2, planes - 1)),
-                dma((modes, 2, planes - 1)),
-                dma((modes, 2, planes - 1)),
-                dma((modes, 2, planes - 1)),
+                dma((4, chunks, 2)),
+                dma((4, chunks, 2)),
+                dma((chunks, 2, planes - 1)),
+                dma((chunks, 2, planes - 1)),
+                dma((chunks, 2, planes - 1)),
+                dma((chunks, 2, planes - 1)),
                 dma((size // TILE,)),
                 dma((size // TILE,)),
                 dma((devices - 1,)),
@@ -721,7 +721,7 @@
                 dma,
             ],
             compiler_params=pltpu.CompilerParams(
-                vmem_limit_bytes=60 * 1024 * 1024, collective_id=0, has_side_effects=True
+                vmem_limit_bytes=56 * 1024 * 1024, collective_id=0, has_side_effects=True
             ),
         )(strip_of, pos_row, pos_col, object_field, probe, amplitude[0], forward, inverse)
         return (strip_grad, term.astype(F32))

time: 164 us -> 138 us (0.84)
  Pallas kernels: 153 us -> 130 us
  other arithmetic: 6.8 us -> 4.56 us
    pallas_call x1, Pallas kernels: 153 us -> 130 us  [shards(): pl.pallas_call(core_kernel, out_shape=(vmem((modes, 2, size, size), BF16)...]
    convert_element_type x1, other arithmetic: 6.8 us -> 4.56 us  [shards(): return (strip_grad, term.astype(F32))]
where the time goes in v5:
time: 138 us
  Pallas kernels  130 us (94%)
  other arithmetic  4.56 us (3%)
  between operations  2.58 us (2%)
    pallas_call x1, Pallas kernels, shards(): pl.pallas_call(core_kernel, out_shape=(vmem((modes, 2, size, size), BF16)...  130 us
    convert_element_type x1, other arithmetic, shards(): return (strip_grad, term.astype(F32))  4.56 us

profile of v5, /device:TPU:0, one launch (start us, length us, event | category | flops | bytes accessed | tf_op | source)
XLA Modules:
  0.0 138.0 jit_solution(5118030596521075057)
XLA Ops:
  2.6 130.1 %shard_map.95 = (bf16[4,2,512,512]{3,2,1,0:T(8,128)(2,1)S(1)}, f32[2,40,1152]{2,1,0:T(8,128)S(1)}) custom-call(s32[1]{0:T(128)S(6)} %copy.14.strip_of, s32[1]{0:T(128)S(6)} %copy.12.row, s32[1]{0:T(128)S(6)} %copy.13.col, f32[2,40,1152]{2,1,0:T(8,128)} %field.1, f32[4,2,512,512]{3,2,1,0:T(8,128)} %probe_hbm.1, f32[512,512]{1,0:T(8,128)} %bitcast.1, ...), custom_call_target="tpu_custom_call" | custom-call | tf_op jit(solution)/shard_map/pallas_call | solution.py:668
  132.7 0.7 copy.11
  133.5 4.6 %convert_element_type.3 = f32[4,2,512,512]{3,2,1,0:T(8,128)} convert(bf16[4,2,512,512]{3,2,1,0:T(8,128)(2,1)S(1)} %get-tuple-element.5) | non-fusion elementwise | flops 2097152 | bytes 12582912 | tf_op jit(solution)/shard_map/convert_element_type | solution.py:727

commit v6 on v5

--- a/solution.py
+++ b/solution.py
@@ -16,13 +16,15 @@
 PLANE = 4
 TILE = 256
 ORDER = (
-    (0, 0), (0, 1), (0, 2), (1, 0), (1, 1), (0, 3), (0, 4), (2, 0), (2, 1), (1, 2),
-    (1, 3), (0, 5), (3, 0), (1, 4), (2, 2), (3, 1), (0, 6), (4, 0), (3, 2), (4, 1),
-    (2, 4), (1, 6), (4, 2), (1, 5), (2, 3), (0, 7), (5, 2), (3, 4), (3, 3), (1, 7),
-    (2, 6), (4, 4), (4, 3), (5, 1), (2, 5), (7, 0), (5, 4), (5, 3), (2, 7), (3, 6),
-    (3, 7), (3, 5), (5, 0), (4, 6), (8, 0), (5, 6), (4, 5), (4, 7), (8, 1), (8, 2),
-    (5, 5), (5, 7), (9, 0),
+    (0, 0), (0, 1), (0, 2), (1, 0), (0, 3), (1, 1), (0, 4), (2, 0), (1, 2), (1, 3),
+    (0, 5), (0, 6), (3, 0), (2, 1), (1, 4), (0, 7), (2, 3), (9, 0), (10, 0), (2, 2),
+    (1, 5), (4, 0), (2, 4), (3, 1), (3, 3), (5, 0), (3, 4), (4, 1), (4, 3), (10, 1),
+    (3, 2), (1, 7), (4, 4), (2, 5), (5, 3), (6, 0), (1, 6), (4, 2), (7, 0), (5, 4),
+    (5, 1), (6, 3), (3, 5), (2, 7), (6, 4), (2, 6), (6, 1), (5, 2), (4, 5), (7, 3),
+    (3, 7), (3, 6), (7, 4), (5, 5), (4, 7), (7, 1), (4, 6), (6, 2), (5, 7), (6, 5),
+    (5, 6), (10, 2), (6, 7), (6, 6), (7, 5), (7, 6), (7, 7), (7, 2), (11, 0),
 )
+PLANES_FIRST = (2,)
 PARAMS = pltpu.CompilerParams(vmem_limit_bytes=56 * 1024 * 1024)
 VMEM = pl.BlockSpec(memory_space=pltpu.VMEM)
 SMEM = pl.BlockSpec(memory_space=pltpu.SMEM)
@@ -200,25 +202,21 @@
 def core_kernel(
     strip_of, row, col, field, probe_hbm, measured_hbm, left_hbm, right_hbm, result, strip_grad,
     metas, held_a, held_b, col_hot, row_hot, cut, probe, patch, measured, left, right,
-    far, power, power_in, scale, wave, half, term, got1, sum1, got2, sum2, got3,
+    far, power, power_in, scale, wave, half, term, got1, sum1, got2, sum2, got3, sum3, got4,
     grad, grad_in, summed, pieces, landed,
     load, load_probe, meta_send, meta_recv, hop_send, hop_recv, swap_send, swap_recv, send, recv,
-    send_z, recv_z, ship_z, land_z, part_send, part_recv, piece_send, piece_recv, strip_send, strip_recv,
+    part_send, part_recv, piece_send, piece_recv, strip_send, strip_recv,
 ):
     modes, size = probe.shape[0], patch.shape[-1]
     devices = lax.axis_size("scan")
     strip, width = strip_grad.shape[1], strip_grad.shape[2]
-    planes = got3.shape[2] + 1
+    planes = devices // 4
     scan, mode = lax.axis_index("scan"), lax.axis_index("mode")
     z, y, x = scan // 4, lax.rem(scan // 2, 2), lax.rem(scan, 2)
     partner = (scan, 1 - mode)
     peer_x = mesh_peer(scan, mode, planes, 1, 0, 0)
     peer_y = mesh_peer(scan, mode, planes, 0, 1, 0)
-    peers_z = [mesh_peer(scan, mode, planes, 0, 0, k) for k in range(1, planes)]
-    first_peer, second_peer = (peer_x, peer_y), (peer_y, peer_x)
-    first_at, second_at = (x, y), (y, x)
     chunk = size // HALVES
-    h, q, e = chunk // 2, chunk // 4, chunk // 4 // planes
     deep = pieces.shape[0] // devices
 
     barrier = pltpu.get_barrier_semaphore()
@@ -364,69 +362,54 @@
     def place(u):
         return u // HALVES, u % HALVES * chunk
 
-    def copy1(u, c):
+    near, far_z = levels[1] * 4 + plane, levels[2] * 4 + plane
+    along = {"x": (peer_x, x), "y": (peer_y, y), "n": ((near, mode), lax.rem(z, 2)), "f": ((far_z, mode), z // 2)}
+    sums, gots = (None, sum1, sum2, sum3), (None, got1, got2, got3, got4)
+
+    def way(u, c, stage):
+        axes = ("nfxy", "nfyx")[c] if u in PLANES_FIRST else ("xynf", "yxnf")[c]
+        return along[axes[stage - 1]]
+
+    def base(u, c, stage):
+        low = place(u)[1]
+        for s in range(1, stage + 1):
+            low = low + way(u, c, s)[1] * (chunk >> s)
+        return low
+
+    def exchange(u, c, stage):
         m, low = place(u)
-        away = rows(low + (1 - first_at[c]) * h, h, h)
-        return remote(term.at[m, c, away], got1.at[u, c], send.at[0, u, c], recv.at[0, u, c], first_peer[c])
-
-    def copy2(u, c):
-        away = rows((1 - second_at[c]) * q, q, q)
-        return remote(sum1.at[u, c, away], got2.at[u, c], send.at[1, u, c], recv.at[1, u, c], second_peer[c])
-
-    def copy3(u, c, k):
-        away = rows(lax.rem(z + k, planes) * e, e, e)
-        return remote(
-            sum2.at[u, c, away], got3.at[u, c, k - 1], send_z.at[u, c, k - 1], recv_z.at[u, c, k - 1], peers_z[k - 1]
-        )
-
-    def base(u, c):
-        return place(u)[1] + first_at[c] * h + second_at[c] * q
-
-    def copy4(u, c, k):
-        own = result.at[place(u)[0], c, rows(base(u, c) + z * e, e, e)]
-        return remote(own, own, ship_z.at[u, c, k - 1], land_z.at[u, c, k - 1], peers_z[k - 1])
-
-    def copy5(u, c):
-        own = result.at[place(u)[0], c, rows(base(u, c), q, q)]
-        return remote(own, own, send.at[2, u, c], recv.at[2, u, c], second_peer[c])
-
-    def copy6(u, c):
-        m, low = place(u)
-        own = result.at[m, c, rows(low + first_at[c] * h, h, h)]
-        return remote(own, own, send.at[3, u, c], recv.at[3, u, c], first_peer[c])
+        if stage > 4:
+            stage = 9 - stage
+            count = chunk >> stage
+            own = result.at[m, c, rows(base(u, c, stage), count, count)]
+            peer, stage = way(u, c, stage)[0], 9 - stage
+            return remote(own, own, send.at[stage - 1, u, c], recv.at[stage - 1, u, c], peer)
+        peer, bit = way(u, c, stage)
+        count = chunk >> stage
+        away = (1 - bit) * count
+        src = term.at[m, c, rows(low + away, count, count)] if stage == 1 else sums[stage - 1].at[u, c, rows(away, count, count)]
+        return remote(src, gots[stage].at[u, c], send.at[stage - 1, u, c], recv.at[stage - 1, u, c], peer)
 
     def start(stage, u):
         for c in range(2):
-            if stage in (3, 4):
-                for k in range(1, planes):
-                    (copy3, copy4)[stage - 3](u, c, k).start()
-            else:
-                {1: copy1, 2: copy2, 5: copy5, 6: copy6}[stage](u, c).start()
+            exchange(u, c, stage).start()
 
     def finish(stage, u):
         m, low = place(u)
         for c in range(2):
+            exchange(u, c, stage).wait_recv()
+            if stage > 4:
+                continue
+            count, bit = chunk >> stage, way(u, c, stage)[1]
             if stage == 1:
-                copy1(u, c).wait_recv()
-                mine = term[m, c, rows(low + first_at[c] * h, h, h)].astype(F32)
-                sum1[u, c] = (mine + got1[u, c].astype(F32)).astype(BF16)
-            if stage == 2:
-                copy2(u, c).wait_recv()
-                mine = sum1[u, c, rows(second_at[c] * q, q, q)].astype(F32)
-                sum2[u, c] = (mine + got2[u, c].astype(F32)).astype(BF16)
-            if stage == 3:
-                total = sum2[u, c, rows(z * e, e, e)].astype(F32)
-                for k in range(1, planes):
-                    copy3(u, c, k).wait_recv()
-                    total = total + got3[u, c, k - 1].astype(F32)
-                result[m, c, rows(base(u, c) + z * e, e, e)] = total.astype(BF16)
+                mine = term[m, c, rows(low + bit * count, count, count)]
+            else:
+                mine = sums[stage - 1][u, c, rows(bit * count, count, count)]
+            total = (mine.astype(F32) + gots[stage][u, c].astype(F32)).astype(BF16)
             if stage == 4:
-                for k in range(1, planes):
-                    copy4(u, c, k).wait_recv()
-            if stage == 5:
-                copy5(u, c).wait_recv()
-            if stage == 6:
-                copy6(u, c).wait_recv()
+                result[m, c, rows(base(u, c, 4), count, count)] = total
+            else:
+                sums[stage][u, c] = total
 
     def swap(i):
         at = rows(i * TILE, TILE, TILE)
@@ -571,28 +554,22 @@
                 backward(u // HALVES)
             across_back(u // HALVES, u % HALVES)
             start(1, u)
-        elif step < 6:
+        elif step < 8:
             finish(step, u)
             start(step + 1, u)
-        elif step == 7:
+        elif step == 9:
             cut_pieces()
-        elif step == 8:
+        elif step == 10:
             for k in range(1 + u, devices, 3):
                 piece(k).start()
         else:
             add_pieces()
 
-    def drain(u):
+    for u in range(modes * HALVES):
+        finish(8, u)
         for c in range(2):
-            for copy in (copy1, copy2, copy5, copy6):
-                copy(u, c).wait_send()
-            for k in range(1, planes):
-                copy3(u, c, k).wait_send()
-                copy4(u, c, k).wait_send()
-
-    for u in range(modes * HALVES):
-        finish(6, u)
-        drain(u)
+            for stage in range(1, 9):
+                exchange(u, c, stage).wait_send()
     for i in range(size // TILE):
         swap(i).wait_send()
         part(i).wait_send()
@@ -662,7 +639,6 @@
     if fits and rows % 8 == 0 and devices * deep % TILE == 0 and devices * deep <= 2 * size:
         dma = pltpu.SemaphoreType.DMA
         chunks, chunk = modes * HALVES, size // HALVES
-        h, q, e = chunk // 2, chunk // 4, chunk // 4 // planes
         vmem, lanes = pltpu.VMEM, (cols // LANES + 1) // 2 * LANES
         any_space = pl.BlockSpec(memory_space=pl.ANY)
         term, strip_grad = pl.pallas_call(
@@ -689,11 +665,13 @@
                 vmem((2 * size, size), BF16),
                 vmem((size, 2 * size), BF16),
                 vmem((modes, 2, size, size), BF16),
-                vmem((chunks, 2, h, size), BF16),
-                vmem((chunks, 2, h, size), BF16),
-                vmem((chunks, 2, q, size), BF16),
-                vmem((chunks, 2, q, size), BF16),
-                vmem((chunks, 2, planes - 1, e, size), BF16),
+                vmem((chunks, 2, chunk // 2, size), BF16),
+                vmem((chunks, 2, chunk // 2, size), BF16),
+                vmem((chunks, 2, chunk // 4, size), BF16),
+                vmem((chunks, 2, chunk // 4, size), BF16),
+                vmem((chunks, 2, chunk // 8, size), BF16),
+                vmem((chunks, 2, chunk // 8, size), BF16),
+                vmem((chunks, 2, chunk // 16, size), BF16),
                 vmem((2, size, size), F32),
                 vmem((size, size), F32),
                 vmem((size, size), BF16),
@@ -707,12 +685,8 @@
                 dma((5, 2, planes)),
                 dma((size // TILE,)),
                 dma((size // TILE,)),
-                dma((4, chunks, 2)),
-                dma((4, chunks, 2)),
-                dma((chunks, 2, planes - 1)),
-                dma((chunks, 2, planes - 1)),
-                dma((chunks, 2, planes - 1)),
-                dma((chunks, 2, planes - 1)),
+                dma((8, chunks, 2)),
+                dma((8, chunks, 2)),
                 dma((size // TILE,)),
                 dma((size // TILE,)),
                 dma((devices - 1,)),

time: 138 us -> 135 us (0.978)
  Pallas kernels: 130 us -> 127 us
    pallas_call x1, Pallas kernels: 130 us -> 127 us  [shards(): pl.pallas_call(core_kernel, out_shape=(vmem((modes, 2, size, size), BF16)...]
where the time goes in v6:
time: 135 us
  Pallas kernels  127 us (94%)
  other arithmetic  4.56 us (3%)
  between operations  2.58 us (2%)
    pallas_call x1, Pallas kernels, shards(): pl.pallas_call(core_kernel, out_shape=(vmem((modes, 2, size, size), BF16)...  127 us
    convert_element_type x1, other arithmetic, shards(): return (strip_grad, term.astype(F32))  4.56 us

profile of v6, /device:TPU:0, one launch (start us, length us, event | category | flops | bytes accessed | tf_op | source)
XLA Modules:
  0.0 135.0 jit_solution(7855527224515385941)
XLA Ops:
  2.6 127.1 %shard_map.95 = (bf16[4,2,512,512]{3,2,1,0:T(8,128)(2,1)S(1)}, f32[2,40,1152]{2,1,0:T(8,128)S(1)}) custom-call(s32[1]{0:T(128)S(6)} %copy.14.strip_of, s32[1]{0:T(128)S(6)} %copy.12.row, s32[1]{0:T(128)S(6)} %copy.13.col, f32[2,40,1152]{2,1,0:T(8,128)} %field.1, f32[4,2,512,512]{3,2,1,0:T(8,128)} %probe_hbm.1, f32[512,512]{1,0:T(8,128)} %bitcast.1, ...), custom_call_target="tpu_custom_call" | custom-call | tf_op jit(solution)/shard_map/pallas_call | solution.py:644
  129.7 0.7 copy.11
  130.4 4.6 %convert_element_type.3 = f32[4,2,512,512]{3,2,1,0:T(8,128)} convert(bf16[4,2,512,512]{3,2,1,0:T(8,128)(2,1)S(1)} %get-tuple-element.5) | non-fusion elementwise | flops 2097152 | bytes 12582912 | tf_op jit(solution)/shard_map/convert_element_type | solution.py:701

commit v7 on v6

--- a/solution.py
+++ b/solution.py
@@ -200,11 +200,11 @@
 
 
 def core_kernel(
-    strip_of, row, col, field, probe_hbm, measured_hbm, left_hbm, right_hbm, result, strip_grad,
-    metas, held_a, held_b, col_hot, row_hot, cut, probe, patch, measured, left, right,
+    strip_of, row, col, field_hbm, probe_hbm, measured_hbm, left_hbm, right_hbm, result, strip_grad,
+    field, held_a, held_b, col_hot, row_hot, cut, probe, patch, measured, left, right,
     far, power, power_in, scale, wave, half, term, got1, sum1, got2, sum2, got3, sum3, got4,
     grad, grad_in, summed, pieces, landed,
-    load, load_probe, meta_send, meta_recv, hop_send, hop_recv, swap_send, swap_recv, send, recv,
+    load, load_probe, hop_send, hop_recv, swap_send, swap_recv, send, recv,
     part_send, part_recv, piece_send, piece_recv, strip_send, strip_recv,
 ):
     modes, size = probe.shape[0], patch.shape[-1]
@@ -220,9 +220,14 @@
     deep = pieces.shape[0] // devices
 
     barrier = pltpu.get_barrier_semaphore()
-    everyone = [partner] + [(lax.rem(scan + k, devices), mode) for k in range(1, devices)]
+    levels = (z, z + 1 - 2 * lax.rem(z, 2), z + 2 - 4 * (z // 2), 3 - z)
+    plane, plane_x, plane_y = y * 2 + x, y * 2 + 1 - x, (1 - y) * 2 + x
+    plane_d = (1 - y) * 2 + 1 - x
+    everyone = [partner, peer_x, peer_y] + [(levels[k] * 4 + plane, mode) for k in range(1, planes)]
     for peer in everyone:
         pl.semaphore_signal(barrier, inc=1, device_id=peer, device_id_type=MESH)
+    own_load = pltpu.make_async_copy(field_hbm.at[mode], field, load.at[3])
+    own_load.start()
 
     def probe_load(m):
         return pltpu.make_async_copy(probe_hbm.at[m], probe.at[m], load_probe.at[m])
@@ -242,20 +247,17 @@
         return jnp.where(mask, 1.0, 0.0).astype(BF16)
 
     held, parts_at = (held_a, held_b), (0, held_a.shape[1], width)
-    plane, plane_x, plane_y = y * 2 + x, y * 2 + 1 - x, (1 - y) * 2 + x
-    plane_d = (1 - y) * 2 + 1 - x
-
-    levels = (z, z + 1 - 2 * lax.rem(z, 2), z + 2 - 4 * (z // 2), 3 - z)
 
     def strip_rows(side, k):
         return rows((side * planes + levels[k]) * deep, deep, deep)
 
-    own = jnp.concatenate([field[mode].astype(BF16), jnp.zeros((deep - strip, width), BF16)])
+    which = lax.broadcasted_iota(jnp.int32, (deep - strip, width), 0)
+    numbers = jnp.where(which == 1, lax.rem(col[0], LANES), col[0] // LANES)
+    numbers = jnp.where(which == 0, strip_of[0], numbers).astype(F32)
+    own_load.wait()
+    own = jnp.concatenate([field[...], numbers]).astype(BF16)
     for i in range(2):
         held[i][strip_rows(plane, 0)] = own[:, parts_at[i] : parts_at[i + 1]]
-    which = lax.broadcasted_iota(jnp.int32, (8, LANES), 0)
-    numbers = jnp.where(which == 1, lax.rem(col[0], LANES), col[0] // LANES)
-    metas[scan] = jnp.where(which == 0, strip_of[0], numbers)
     pl.semaphore_wait(barrier, len(everyone))
 
     def remote(src, dst, send_sem, recv_sem, peer):
@@ -263,10 +265,10 @@
             src_ref=src, dst_ref=dst, send_sem=send_sem, recv_sem=recv_sem, device_id=peer, device_id_type=MESH
         )
 
-    def meta(k, back=0):
-        at = lax.rem(scan + devices - back, devices)
-        to = (lax.rem(scan + k, devices), mode)
-        return remote(metas.at[at], metas.at[at], meta_send.at[k - 1], meta_recv.at[k - 1], to)
+    def number(slot, which, lanes):
+        block = held_a[rows(slot * deep + deep - 16, 16, 16), :lanes].astype(F32)
+        at = 16 - (deep - strip) + which
+        return block[at : at + 1].astype(jnp.int32)
 
     def hop(kind, i, k, side, peer):
         at = held[i].at[strip_rows(side, k)]
@@ -287,22 +289,45 @@
         hop(2, 1, k, plane_y, peer_y).wait_recv()
         hop(3, 1, k, plane_y, peer_x).start()
 
-    def cut_columns(side):
-        at = rows(side * planes * deep, planes * deep, planes * deep)
+    def absorb(side, first=False, last=False):
+        taken = planes * deep
+        at = rows(side * taken, taken, taken)
         got = jnp.dot(held_a[at], col_hot[: held_a.shape[1]], preferred_element_type=F32)
         got = got + jnp.dot(held_b[at], col_hot[held_a.shape[1] :], preferred_element_type=F32)
-        cut[at] = got.astype(BF16)
+        cut[...] = got.astype(BF16)
+        lane = lax.broadcasted_iota(jnp.int32, (1, taken), 1)
+        target = jnp.full((1, taken), -1, jnp.int32)
+        for j in range(planes):
+            ahead = lane - j * deep
+            begin = number(side * planes + j, 0, taken) * strip
+            target = jnp.where((ahead >= 0) & (ahead < strip), begin + ahead, target)
+        target = target - row[0]
+
+        def line_hot(i, carry):
+            line = lax.broadcasted_iota(jnp.int32, (64, taken), 0) + i * 64
+            row_hot[rows(i * 64, 64, 64)] = one_hot(line == target)
+            return carry
+
+        lax.fori_loop(0, size // 64, line_hot, 0)
+        for i in range(size // TILE):
+            at = pl.ds(i * TILE, TILE)
+            piled = jnp.dot(row_hot[at], cut[...], preferred_element_type=F32)
+            if not first:
+                piled = power[at] + piled
+            if last:
+                patch[mode, at] = piled.astype(BF16)
+                patch_swap(i).start()
+            else:
+                power[at] = piled
 
     def patch_swap(i):
         at = rows(i * TILE, TILE, TILE)
         own = patch.at[mode, at]
         return remote(own, own, hop_send.at[4, i, 0], hop_recv.at[4, i, 0], partner)
 
-    def across_lanes(row_values, count):
-        return jnp.concatenate([row_values] * (count // LANES), axis=1)
-
-    for k in range(1, devices):
-        meta(k).start()
+    def slot_of(j):
+        return lax.rem(j, 4) * planes + j // 4
+
     for k in range(1, planes):
         hop_z(0, k).start()
         hop_z(1, k).start()
@@ -320,40 +345,18 @@
         hop(0, 1, k, plane, partner).wait_recv()
         spread(k)
         relay(k - 1)
-    cut_columns(plane)
     relay(planes - 1)
-    for k in range(1, devices):
-        meta(k, k).wait_recv()
-    lane = lax.broadcasted_iota(jnp.int32, (8, devices * deep), 1)
-    target = jnp.full((8, devices * deep), -1, jnp.int32)
-    for j in range(devices):
-        ahead = lane - (j % 4 * planes + j // 4) * deep
-        target = jnp.where(
-            (ahead >= 0) & (ahead < strip), across_lanes(metas[j, :1], devices * deep) * strip + ahead, target
-        )
-    target = target[:1] - row[0]
-
-    def line_hot(i, carry):
-        at = rows(i * 64, 64, 64)
-        line = lax.broadcasted_iota(jnp.int32, (64, devices * deep), 0) + i * 64
-        row_hot[at] = one_hot(line == target)
-        return carry
-
-    lax.fori_loop(0, size // 64, line_hot, 0)
+    absorb(plane, first=True)
     for k in range(planes):
         hop(1, 1, k, plane_x, peer_x).wait_recv()
-    cut_columns(plane_x)
+    absorb(plane_x)
     for k in range(planes):
         hop(2, 0, k, plane_y, peer_y).wait_recv()
-    cut_columns(plane_y)
+    absorb(plane_y)
     for k in range(planes):
         hop(3, 0, k, plane_d, peer_y).wait_recv()
         hop(3, 1, k, plane_d, peer_x).wait_recv()
-    cut_columns(plane_d)
-    for i in range(size // TILE):
-        at = pl.ds(i * TILE, TILE)
-        patch[mode, at] = jnp.dot(row_hot[at], cut[...], preferred_element_type=F32).astype(BF16)
-        patch_swap(i).start()
+    absorb(plane_d, last=True)
     for copy in loads:
         copy.wait()
     for i in range(size // TILE):
@@ -446,7 +449,7 @@
         ahead = lax.broadcasted_iota(jnp.int32, (deep, size), 1) - lax.broadcasted_iota(jnp.int32, (deep, size), 0)
 
         def pick(j, carry):
-            begin = across_lanes(metas[j, :1], size) * strip - row[0]
+            begin = number(slot_of(j), 0, size) * strip - row[0]
             wave[rows(j * deep, deep, deep)] = one_hot(ahead == begin)
             return carry
 
@@ -469,7 +472,7 @@
         ahead = ahead - lax.broadcasted_iota(jnp.int32, (LANES, 2 * LANES), 0)
 
         def one(j, carry):
-            turn = one_hot(ahead == across_lanes(metas[j, 1:2], 2 * LANES))
+            turn, whole_lanes = one_hot(ahead == number(slot_of(j), 1, 2 * LANES)), number(slot_of(j), 2, LANES)
             blocks = jnp.concatenate(
                 [landed[rows(j * deep, deep, deep), b * LANES : (b + 1) * LANES] for b in range(parts)]
             )
@@ -481,7 +484,7 @@
                 for t in range((width - size) // LANES + 1):
                     if b + t < width // LANES:
                         to = slice((b + t) * LANES, (b + t + 1) * LANES)
-                        strip_grad[mode, :, to] += jnp.where(metas[j, 2:3] == t, here, 0.0)
+                        strip_grad[mode, :, to] += jnp.where(whole_lanes == t, here, 0.0)
             return carry
 
         lax.fori_loop(0, devices, one, 0)
@@ -578,8 +581,6 @@
     strip_swap().wait()
     for i in range(size // TILE):
         patch_swap(i).wait_send()
-    for k in range(1, devices):
-        meta(k).wait_send()
     for i in range(2):
         for k in range(planes):
             if k:
@@ -589,6 +590,24 @@
             hop(3, i, k, (plane_x, plane_y)[i], (peer_y, peer_x)[i]).wait_send()
 
 
+def cast_kernel(summed, strips, wide, strip_grad, block, done, strip_done):
+    modes, depth = summed.shape[0], block.shape[0]
+    last = pltpu.make_async_copy(strips, strip_grad, strip_done)
+    last.start()
+
+    def out(i):
+        return pltpu.make_async_copy(block.at[i % depth], wide.at[i // 2, i % 2], done.at[i % depth])
+
+    for i in range(2 * modes):
+        if i >= depth:
+            out(i - depth).wait()
+        block[i % depth] = summed[i // 2, i % 2].astype(F32)
+        out(i).start()
+    for i in range(max(2 * modes - depth, 0), 2 * modes):
+        out(i).wait()
+    last.wait()
+
+
 def place_kernel(strips, row, grad, out, padded):
     count, parts, rows, size = out.shape
     padded[...] = jnp.zeros_like(padded)
@@ -636,6 +655,7 @@
     planes, deep = devices // 4, -(-rows // 16) * 16
     fits = groups == 2 and devices == 4 * planes and planes == 4 and size % (64 * HALVES * planes) == 0 and modes * HALVES == 8
     fits = fits and cols % LANES == 0 and size // TILE == 2
+    fits = fits and deep - rows >= 8
     if fits and rows % 8 == 0 and devices * deep % TILE == 0 and devices * deep <= 2 * size:
         dma = pltpu.SemaphoreType.DMA
         chunks, chunk = modes * HALVES, size // HALVES
@@ -644,15 +664,15 @@
         term, strip_grad = pl.pallas_call(
             core_kernel,
             out_shape=(vmem((modes, 2, size, size), BF16), vmem((2, rows, cols), F32)),
-            in_specs=[SMEM] * 3 + [VMEM] + [any_space] * 4,
+            in_specs=[SMEM] * 3 + [any_space] * 5,
             out_specs=(VMEM, VMEM),
             scratch_shapes=[
-                vmem((devices, 8, LANES), jnp.int32),
+                vmem((rows, cols), F32),
                 vmem((devices * deep, lanes), BF16),
                 vmem((devices * deep, cols - lanes), BF16),
                 vmem((cols, size), BF16),
-                vmem((size, devices * deep), BF16),
-                vmem((devices * deep, size), BF16),
+                vmem((size, planes * deep), BF16),
+                vmem((planes * deep, size), BF16),
                 vmem((modes, 2, size, size), F32),
                 vmem((2, size, size), BF16),
                 vmem((size, size), F32),
@@ -677,10 +697,8 @@
                 vmem((size, size), BF16),
                 vmem((devices * deep, size), BF16),
                 vmem((devices * deep, size), BF16),
-                dma((3,)),
+                dma((4,)),
                 dma((modes,)),
-                dma((devices - 1,)),
-                dma((devices - 1,)),
                 dma((5, 2, planes)),
                 dma((5, 2, planes)),
                 dma((size // TILE,)),
@@ -698,7 +716,15 @@
                 vmem_limit_bytes=56 * 1024 * 1024, collective_id=0, has_side_effects=True
             ),
         )(strip_of, pos_row, pos_col, object_field, probe, amplitude[0], forward, inverse)
-        return (strip_grad, term.astype(F32))
+        probe_grad, strip_grad = pl.pallas_call(
+            cast_kernel,
+            out_shape=(jax.ShapeDtypeStruct(term.shape, F32), jax.ShapeDtypeStruct(strip_grad.shape, F32)),
+            in_specs=[VMEM] * 2,
+            out_specs=(any_space, any_space),
+            scratch_shapes=[vmem((4, size, size), F32), dma((4,)), dma],
+            compiler_params=pltpu.CompilerParams(vmem_limit_bytes=16 * 1024 * 1024),
+        )(pltpu.with_memory_space_constraint(term, vmem), pltpu.with_memory_space_constraint(strip_grad, vmem))
+        return (strip_grad, probe_grad)
 
     lane = lax.broadcasted_iota(jnp.int32, (2, META, cols), 2)
     numbers = jnp.where(lane == 0, strip_of[0], jnp.where(lane == 1, pos_col[0] // LANES, pos_col[0] % LANES))

time: 135 us -> 132 us (0.978)
  other arithmetic: 4.56 us -> 0 us
  Pallas kernels: 127 us -> 129 us
    convert_element_type x1 -> x0, other arithmetic: 4.56 us -> none  [shards(): return (strip_grad, term.astype(F32))]
    pallas_call x0 -> x1, Pallas kernels: none -> 3.46 us  [shards(): pl.pallas_call(cast_kernel, out_shape=(jax.ShapeDtypeStruct(term.shape, F...]
    pallas_call x1, Pallas kernels: 127 us -> 125 us  [shards(): pl.pallas_call(core_kernel, out_shape=(vmem((modes, 2, size, size), BF16)...]
where the time goes in v7:
time: 132 us; the launch traced here: 131 us
  Pallas kernels  129 us (98%)
  between operations  2.74 us (2%)
    pallas_call x1, Pallas kernels, shards(): pl.pallas_call(core_kernel, out_shape=(vmem((modes, 2, size, size), BF16)...  125 us
    pallas_call x1, Pallas kernels, shards(): pl.pallas_call(cast_kernel, out_shape=(jax.ShapeDtypeStruct(term.shape, F...  3.46 us

profile of v7, /device:TPU:0, one launch (start us, length us, event | category | flops | bytes accessed | tf_op | source)
XLA Modules:
  0.0 131.5 jit_solution(8946490025953057279)
XLA Ops:
  2.6 125.3 %shard_map.95 = (bf16[4,2,512,512]{3,2,1,0:T(8,128)(2,1)S(1)}, f32[2,40,1152]{2,1,0:T(8,128)S(1)}) custom-call(s32[1]{0:T(128)S(6)} %copy.12.strip_of, s32[1]{0:T(128)S(6)} %copy.10.row, s32[1]{0:T(128)S(6)} %copy.11.col, f32[2,40,1152]{2,1,0:T(8,128)} %field_hbm.1, f32[4,2,512,512]{3,2,1,0:T(8,128)} %probe_hbm.1, f32[512,512]{1,0:T(8,128)} %bitcast.1, ...), custom_call_target="tpu_custom_call" | custom-call | tf_op jit(solution)/shard_map/pallas_call | solution.py:664
  127.9 3.5 %shard_map.96 = (f32[4,2,512,512]{3,2,1,0:T(8,128)}, f32[2,40,1152]{2,1,0:T(8,128)}) custom-call(bf16[4,2,512,512]{3,2,1,0:T(8,128)(2,1)S(1)} %get-tuple-element.6.summed, f32[2,40,1152]{2,1,0:T(8,128)S(1)} %get-tuple-element.7.strips), custom_call_target="tpu_custom_call" | custom-call | tf_op jit(solution)/shard_map/pallas_call | solution.py:719

commit v8 on v7

--- a/solution.py
+++ b/solution.py
@@ -16,15 +16,17 @@
 PLANE = 4
 TILE = 256
 ORDER = (
-    (0, 0), (0, 1), (0, 2), (1, 0), (0, 3), (1, 1), (0, 4), (2, 0), (1, 2), (1, 3),
-    (0, 5), (0, 6), (3, 0), (2, 1), (1, 4), (0, 7), (2, 3), (9, 0), (10, 0), (2, 2),
-    (1, 5), (4, 0), (2, 4), (3, 1), (3, 3), (5, 0), (3, 4), (4, 1), (4, 3), (10, 1),
-    (3, 2), (1, 7), (4, 4), (2, 5), (5, 3), (6, 0), (1, 6), (4, 2), (7, 0), (5, 4),
-    (5, 1), (6, 3), (3, 5), (2, 7), (6, 4), (2, 6), (6, 1), (5, 2), (4, 5), (7, 3),
-    (3, 7), (3, 6), (7, 4), (5, 5), (4, 7), (7, 1), (4, 6), (6, 2), (5, 7), (6, 5),
-    (5, 6), (10, 2), (6, 7), (6, 6), (7, 5), (7, 6), (7, 7), (7, 2), (11, 0),
+    (0, 0), (0, 1), (0, 2), (0, 3), (1, 0), (1, 1), (0, 4), (1, 3), (0, 5), (2, 1),
+    (1, 2), (0, 6), (1, 4), (0, 7), (2, 3), (3, 1), (9, 0), (1, 5), (2, 0), (3, 3),
+    (10, 1), (10, 2), (4, 1), (2, 4), (2, 2), (4, 3), (1, 6), (10, 3), (10, 4), (10, 5),
+    (2, 5), (5, 1), (3, 4), (5, 3), (1, 7), (3, 0), (3, 5), (6, 1), (10, 6), (10, 7),
+    (10, 8), (3, 2), (2, 7), (6, 3), (4, 5), (2, 6), (4, 4), (7, 1), (4, 2), (4, 0),
+    (3, 7), (7, 3), (5, 5), (3, 6), (5, 4), (10, 9), (10, 10), (5, 0), (5, 2), (6, 5),
+    (4, 7), (4, 6), (6, 4), (10, 11), (10, 12), (7, 5), (6, 0), (5, 7), (5, 6), (7, 4),
+    (6, 2), (6, 7), (10, 13), (10, 14), (10, 15), (6, 6), (7, 0), (7, 2), (7, 7), (7, 6),
+    (11, 0),
 )
-PLANES_FIRST = (2,)
+PLANES_FIRST = ((2, 0), (2, 1), (0, 1))
 PARAMS = pltpu.CompilerParams(vmem_limit_bytes=56 * 1024 * 1024)
 VMEM = pl.BlockSpec(memory_space=pltpu.VMEM)
 SMEM = pl.BlockSpec(memory_space=pltpu.SMEM)
@@ -217,7 +219,7 @@
     peer_x = mesh_peer(scan, mode, planes, 1, 0, 0)
     peer_y = mesh_peer(scan, mode, planes, 0, 1, 0)
     chunk = size // HALVES
-    deep = pieces.shape[0] // devices
+    deep, tall = held_a.shape[0] // devices, pieces.shape[0] // devices
 
     barrier = pltpu.get_barrier_semaphore()
     levels = (z, z + 1 - 2 * lax.rem(z, 2), z + 2 - 4 * (z // 2), 3 - z)
@@ -370,7 +372,7 @@
     sums, gots = (None, sum1, sum2, sum3), (None, got1, got2, got3, got4)
 
     def way(u, c, stage):
-        axes = ("nfxy", "nfyx")[c] if u in PLANES_FIRST else ("xynf", "yxnf")[c]
+        axes = ("nfxy", "nfyx")[c] if (u, c) in PLANES_FIRST else ("xynf", "yxnf")[c]
         return along[axes[stage - 1]]
 
     def base(u, c, stage):
@@ -427,15 +429,15 @@
         at = rows(i * TILE, TILE, TILE)
         return remote(grad.at[1 - mode, at], grad_in.at[at], part_send.at[i], part_recv.at[i], partner)
 
-    mine = rows(scan * deep, deep, deep)
+    mine = rows(scan * tall, tall, 16)
 
     def piece(k):
         to = lax.rem(scan + k, devices)
-        return remote(pieces.at[rows(to * deep, deep, deep)], landed.at[mine], piece_send.at[k - 1], piece_recv.at[k - 1], (to, mode))
+        return remote(pieces.at[rows(to * tall, tall, 16)], landed.at[mine], piece_send.at[k - 1], piece_recv.at[k - 1], (to, mode))
 
     def arrive(k):
         come = lax.rem(scan + devices - k, devices)
-        at = rows(come * deep, deep, deep)
+        at = rows(come * tall, tall, 16)
         return remote(pieces.at[at], landed.at[at], piece_send.at[k - 1], piece_recv.at[k - 1], (come, mode))
 
     def strip_swap():
@@ -446,21 +448,25 @@
             part(i).wait_recv()
             at = pl.ds(i * TILE, TILE)
             summed[at] = (grad[mode, at] + grad_in[at]).astype(BF16)
-        ahead = lax.broadcasted_iota(jnp.int32, (deep, size), 1) - lax.broadcasted_iota(jnp.int32, (deep, size), 0)
-
-        def pick(j, carry):
-            begin = number(slot_of(j), 0, size) * strip - row[0]
-            wave[rows(j * deep, deep, deep)] = one_hot(ahead == begin)
+        down = lax.broadcasted_iota(jnp.int32, (tall, size), 0)
+        ahead = lax.broadcasted_iota(jnp.int32, (tall, size), 1) - jnp.where(down < strip, down, down - strip)
+
+        def pick(i, carry):
+            begins = [number(slot_of(2 * i + j), 0, size) * strip - row[0] for j in range(2)]
+            wave[rows(i * tall, tall, 16)] = one_hot(ahead == jnp.where(down < strip, begins[0], begins[1]))
             return carry
 
-        lax.fori_loop(0, devices, pick, 0)
+        lax.fori_loop(0, devices // 2, pick, 0)
 
         def move(i, carry):
-            at = rows(i * TILE, TILE, TILE)
-            pieces[at] = jnp.dot(wave[at], summed[...], preferred_element_type=F32).astype(BF16)
+            out = jnp.dot(wave[rows(i * 4 * tall, 4 * tall, 16)], summed[...], preferred_element_type=F32)
+            for j in range(8):
+                block = out[j * strip : (j + 1) * strip]
+                block = jnp.concatenate([block[:, : size // 2], block[:, size // 2 :]])
+                pieces[rows((i * 8 + j) * tall, tall, 16)] = block.astype(BF16)
             return carry
 
-        lax.fori_loop(0, devices * deep // TILE, move, 0)
+        lax.fori_loop(0, devices // 8, move, 0)
         landed[mine] = pieces[mine]
 
     def add_pieces():
@@ -473,14 +479,19 @@
 
         def one(j, carry):
             turn, whole_lanes = one_hot(ahead == number(slot_of(j), 1, 2 * LANES)), number(slot_of(j), 2, LANES)
+            piece_rows = landed[rows(j * tall, tall, 16)].astype(F32)
             blocks = jnp.concatenate(
-                [landed[rows(j * deep, deep, deep), b * LANES : (b + 1) * LANES] for b in range(parts)]
-            )
+                [
+                    piece_rows[b * strip : (b + 1) * strip, at * LANES : (at + 1) * LANES]
+                    for b in range(2)
+                    for at in range(parts // 2)
+                ]
+            ).astype(BF16)
             moved = jnp.dot(blocks, turn, preferred_element_type=F32)
             for b in range(parts + 1):
-                here = moved[b * deep : b * deep + strip, :LANES] if b < parts else 0.0
+                here = moved[b * strip : (b + 1) * strip, :LANES] if b < parts else 0.0
                 if b > 0:
-                    here = here + moved[(b - 1) * deep : (b - 1) * deep + strip, LANES:]
+                    here = here + moved[(b - 1) * strip : b * strip, LANES:]
                 for t in range((width - size) // LANES + 1):
                     if b + t < width // LANES:
                         to = slice((b + t) * LANES, (b + t + 1) * LANES)
@@ -563,8 +574,7 @@
         elif step == 9:
             cut_pieces()
         elif step == 10:
-            for k in range(1 + u, devices, 3):
-                piece(k).start()
+            piece(u).start()
         else:
             add_pieces()
 
@@ -656,6 +666,7 @@
     fits = groups == 2 and devices == 4 * planes and planes == 4 and size % (64 * HALVES * planes) == 0 and modes * HALVES == 8
     fits = fits and cols % LANES == 0 and size // TILE == 2
     fits = fits and deep - rows >= 8
+    fits = fits and 2 * rows % 16 == 0 and size % (2 * LANES) == 0
     if fits and rows % 8 == 0 and devices * deep % TILE == 0 and devices * deep <= 2 * size:
         dma = pltpu.SemaphoreType.DMA
         chunks, chunk = modes * HALVES, size // HALVES
@@ -695,8 +706,8 @@
                 vmem((2, size, size), F32),
                 vmem((size, size), F32),
                 vmem((size, size), BF16),
-                vmem((devices * deep, size), BF16),
-                vmem((devices * deep, size), BF16),
+                vmem((devices * 2 * rows, size // 2), BF16),
+                vmem((devices * 2 * rows, size // 2), BF16),
                 dma((4,)),
                 dma((modes,)),
                 dma((5, 2, planes)),

time: 132 us -> 126 us (0.955)
  Pallas kernels: 129 us -> 123 us
    pallas_call x1, Pallas kernels: 125 us -> 120 us  [shards(): pl.pallas_call(core_kernel, out_shape=(vmem((modes, 2, size, size), BF16)...]
where the time goes in v8:
time: 126 us
  Pallas kernels  123 us (98%)
  between operations  2.74 us (2%)
    pallas_call x1, Pallas kernels, shards(): pl.pallas_call(core_kernel, out_shape=(vmem((modes, 2, size, size), BF16)...  120 us
    pallas_call x1, Pallas kernels, shards(): pl.pallas_call(cast_kernel, out_shape=(jax.ShapeDtypeStruct(term.shape, F...  3.46 us

profile of v8, /device:TPU:0, one launch (start us, length us, event | category | flops | bytes accessed | tf_op | source)
XLA Modules:
  0.0 126.1 jit_solution(8207721762315242900)
XLA Ops:
  2.6 119.9 %shard_map.95 = (bf16[4,2,512,512]{3,2,1,0:T(8,128)(2,1)S(1)}, f32[2,40,1152]{2,1,0:T(8,128)S(1)}) custom-call(s32[1]{0:T(128)S(6)} %copy.12.strip_of, s32[1]{0:T(128)S(6)} %copy.10.row, s32[1]{0:T(128)S(6)} %copy.11.col, f32[2,40,1152]{2,1,0:T(8,128)} %field_hbm.1, f32[4,2,512,512]{3,2,1,0:T(8,128)} %probe_hbm.1, f32[512,512]{1,0:T(8,128)} %bitcast.1, ...), custom_call_target="tpu_custom_call" | custom-call | tf_op jit(solution)/shard_map/pallas_call | solution.py:675
  122.5 3.5 %shard_map.96 = (f32[4,2,512,512]{3,2,1,0:T(8,128)}, f32[2,40,1152]{2,1,0:T(8,128)}) custom-call(bf16[4,2,512,512]{3,2,1,0:T(8,128)(2,1)S(1)} %get-tuple-element.6.summed, f32[2,40,1152]{2,1,0:T(8,128)S(1)} %get-tuple-element.7.strips), custom_call_target="tpu_custom_call" | custom-call | tf_op jit(solution)/shard_map/pallas_call | solution.py:730

commit v9 on v8

--- a/solution.py
+++ b/solution.py
@@ -16,17 +16,17 @@
 PLANE = 4
 TILE = 256
 ORDER = (
-    (0, 0), (0, 1), (0, 2), (0, 3), (1, 0), (1, 1), (0, 4), (1, 3), (0, 5), (2, 1),
-    (1, 2), (0, 6), (1, 4), (0, 7), (2, 3), (3, 1), (9, 0), (1, 5), (2, 0), (3, 3),
-    (10, 1), (10, 2), (4, 1), (2, 4), (2, 2), (4, 3), (1, 6), (10, 3), (10, 4), (10, 5),
-    (2, 5), (5, 1), (3, 4), (5, 3), (1, 7), (3, 0), (3, 5), (6, 1), (10, 6), (10, 7),
-    (10, 8), (3, 2), (2, 7), (6, 3), (4, 5), (2, 6), (4, 4), (7, 1), (4, 2), (4, 0),
-    (3, 7), (7, 3), (5, 5), (3, 6), (5, 4), (10, 9), (10, 10), (5, 0), (5, 2), (6, 5),
-    (4, 7), (4, 6), (6, 4), (10, 11), (10, 12), (7, 5), (6, 0), (5, 7), (5, 6), (7, 4),
-    (6, 2), (6, 7), (10, 13), (10, 14), (10, 15), (6, 6), (7, 0), (7, 2), (7, 7), (7, 6),
+    (0, 0), (0, 1), (0, 2), (0, 3), (1, 0), (1, 1), (0, 4), (1, 2), (0, 5), (2, 1),
+    (1, 3), (0, 6), (1, 4), (3, 1), (0, 7), (2, 2), (9, 0), (10, 1), (2, 0), (3, 2),
+    (2, 3), (10, 2), (10, 3), (4, 1), (10, 4), (2, 4), (10, 5), (4, 2), (10, 6), (3, 4),
+    (10, 7), (1, 7), (5, 1), (1, 5), (3, 0), (10, 8), (3, 3), (5, 2), (1, 6), (2, 7),
+    (6, 1), (4, 4), (2, 5), (4, 3), (6, 2), (4, 0), (3, 7), (2, 6), (10, 9), (7, 1),
+    (3, 5), (7, 2), (5, 4), (10, 10), (4, 7), (3, 6), (4, 5), (6, 4), (5, 0), (10, 11),
+    (5, 7), (5, 3), (10, 12), (4, 6), (7, 4), (5, 5), (6, 0), (6, 7), (10, 13), (5, 6),
+    (6, 3), (10, 14), (6, 5), (10, 15), (7, 0), (6, 6), (7, 5), (7, 3), (7, 6), (7, 7),
     (11, 0),
 )
-PLANES_FIRST = ((2, 0), (2, 1), (0, 1))
+PLANES_FIRST = ((3, 0), (3, 1), (0, 1))
 PARAMS = pltpu.CompilerParams(vmem_limit_bytes=56 * 1024 * 1024)
 VMEM = pl.BlockSpec(memory_space=pltpu.VMEM)
 SMEM = pl.BlockSpec(memory_space=pltpu.SMEM)
@@ -286,10 +286,11 @@
             hop(2, 1 - i, k, plane, peer_y).start()
 
     def relay(k):
-        hop(1, 0, k, plane_x, peer_x).wait_recv()
-        hop(3, 0, k, plane_x, peer_y).start()
-        hop(2, 1, k, plane_y, peer_y).wait_recv()
-        hop(3, 1, k, plane_y, peer_x).start()
+        i = 0 if k < planes // 2 else 1
+        hop(1, i, k, plane_x, peer_x).wait_recv()
+        hop(3, i, k, plane_x, peer_y).start()
+        hop(2, 1 - i, k, plane_y, peer_y).wait_recv()
+        hop(3, 1 - i, k, plane_y, peer_x).start()
 
     def absorb(side, first=False, last=False):
         taken = planes * deep
@@ -350,10 +351,10 @@
     relay(planes - 1)
     absorb(plane, first=True)
     for k in range(planes):
-        hop(1, 1, k, plane_x, peer_x).wait_recv()
+        hop(1, int(k < planes // 2), k, plane_x, peer_x).wait_recv()
     absorb(plane_x)
     for k in range(planes):
-        hop(2, 0, k, plane_y, peer_y).wait_recv()
+        hop(2, int(k >= planes // 2), k, plane_y, peer_y).wait_recv()
     absorb(plane_y)
     for k in range(planes):
         hop(3, 0, k, plane_d, peer_y).wait_recv()
@@ -501,21 +502,22 @@
         lax.fori_loop(0, devices, one, 0)
         strip_swap().start()
 
+    def leave(m, at, low):
+        pr, pi, xr, xi = probe[m, 0, at], probe[m, 1, at], patch[0, at].astype(F32), patch[1, at].astype(F32)
+        wave[at] = (pr * xr - pi * xi).astype(BF16)
+        wave[low] = (pr * xi + pi * xr).astype(BF16)
+
     def forward(m, carry):
-        probe_load(m).wait()
-
-        def leave(i, carry):
-            at, low = rows(i * 64, 64, 64), rows(size + i * 64, 64, 64)
-            pr, pi, xr, xi = probe[m, 0, at], probe[m, 1, at], patch[0, at].astype(F32), patch[1, at].astype(F32)
-            wave[at] = (pr * xr - pi * xi).astype(BF16)
-            wave[low] = (pr * xi + pi * xr).astype(BF16)
-            return carry
-
-        lax.fori_loop(0, size // 64, leave, 0)
+        @pl.when(m < modes - 1)
+        def _():
+            probe_load(m + 1).wait()
+
         product(left, wave)
+        after = jnp.minimum(m + 1, modes - 1)
 
         def across(i, carry):
             at = rows(i * TILE, TILE, TILE)
+            leave(after, at, rows(size + i * TILE, TILE, TILE))
             both = jnp.dot(half[at], right[...], preferred_element_type=F32)
             re, im = both[:, :size], both[:, size:]
             far[m, 0, at] = re
@@ -532,6 +534,12 @@
         lax.fori_loop(0, size // TILE, across, 0)
         return carry
 
+    def first_leave(i, carry):
+        leave(0, rows(i * 64, 64, 64), rows(size + i * 64, 64, 64))
+        return carry
+
+    probe_load(0).wait()
+    lax.fori_loop(0, size // 64, first_leave, 0)
     lax.fori_loop(0, modes, forward, 0)
     for i in range(size // TILE):
         at = pl.ds(i * TILE, TILE)
@@ -539,18 +547,24 @@
         total = jnp.maximum(power[at] + power_in[at], 0.25)
         scale[at] = 1.0 - measured[at] / jnp.sqrt(total)
 
+    def residual(m, at, low):
+        wave[at] = (far[m, 0, at] * scale[at]).astype(BF16)
+        wave[low] = (far[m, 1, at] * scale[at]).astype(BF16)
+
     def backward(m):
-        def residual(i, carry):
-            at, low = rows(i * 64, 64, 64), rows(size + i * 64, 64, 64)
-            wave[at] = (far[m, 0, at] * scale[at]).astype(BF16)
-            wave[low] = (far[m, 1, at] * scale[at]).astype(BF16)
-            return carry
-
-        lax.fori_loop(0, size // 64, residual, 0)
+        if m == 0:
+
+            def first_residual(i, carry):
+                residual(0, rows(i * 64, 64, 64), rows(size + i * 64, 64, 64))
+                return carry
+
+            lax.fori_loop(0, size // 64, first_residual, 0)
         product(right, wave)
 
     def across_back(m, i):
         at = pl.ds(i * TILE, TILE)
+        if m < modes - 1:
+            residual(m + 1, at, pl.ds(size + i * TILE, TILE))
         both = jnp.dot(half[at], left[...], preferred_element_type=F32)
         br, bi = both[:, :size], both[:, size:]
         pr, pi, xr, xi = probe[m, 0, at], probe[m, 1, at], patch[0, at].astype(F32), patch[1, at].astype(F32)
@@ -597,7 +611,8 @@
                 hop_z(i, k).wait_send()
             hop(1, i, k, plane, peer_x).wait_send()
             hop(2, i, k, plane, peer_y).wait_send()
-            hop(3, i, k, (plane_x, plane_y)[i], (peer_y, peer_x)[i]).wait_send()
+            swapped = i if k < planes // 2 else 1 - i
+            hop(3, i, k, (plane_x, plane_y)[swapped], (peer_y, peer_x)[swapped]).wait_send()
 
 
 def cast_kernel(summed, strips, wide, strip_grad, block, done, strip_done):

time: 126 us -> 132 us (1.048)
  Pallas kernels: 123 us -> 129 us
    pallas_call x1, Pallas kernels: 120 us -> 126 us  [shards(): pl.pallas_call(core_kernel, out_shape=(vmem((modes, 2, size, size), BF16)...]
where the time goes in v9:
time: 132 us
  Pallas kernels  129 us (98%)
  between operations  2.74 us (2%)
    pallas_call x1, Pallas kernels, shards(): pl.pallas_call(core_kernel, out_shape=(vmem((modes, 2, size, size), BF16)...  126 us
    pallas_call x1, Pallas kernels, shards(): pl.pallas_call(cast_kernel, out_shape=(jax.ShapeDtypeStruct(term.shape, F...  3.46 us

profile of v9, /device:TPU:0, one launch (start us, length us, event | category | flops | bytes accessed | tf_op | source)
XLA Modules:
  0.0 132.2 jit_solution(8386136605209563167)
XLA Ops:
  2.6 126.0 %shard_map.95 = (bf16[4,2,512,512]{3,2,1,0:T(8,128)(2,1)S(1)}, f32[2,40,1152]{2,1,0:T(8,128)S(1)}) custom-call(s32[1]{0:T(128)S(6)} %copy.12.strip_of, s32[1]{0:T(128)S(6)} %copy.10.row, s32[1]{0:T(128)S(6)} %copy.11.col, f32[2,40,1152]{2,1,0:T(8,128)} %field_hbm.1, f32[4,2,512,512]{3,2,1,0:T(8,128)} %probe_hbm.1, f32[512,512]{1,0:T(8,128)} %bitcast.1, ...), custom_call_target="tpu_custom_call" | custom-call | tf_op jit(solution)/shard_map/pallas_call | solution.py:690
  128.6 3.5 %shard_map.96 = (f32[4,2,512,512]{3,2,1,0:T(8,128)}, f32[2,40,1152]{2,1,0:T(8,128)}) custom-call(bf16[4,2,512,512]{3,2,1,0:T(8,128)(2,1)S(1)} %get-tuple-element.6.summed, f32[2,40,1152]{2,1,0:T(8,128)S(1)} %get-tuple-element.7.strips), custom_call_target="tpu_custom_call" | custom-call | tf_op jit(solution)/shard_map/pallas_call | solution.py:745

commit v10 on v8

--- a/solution.py
+++ b/solution.py
@@ -16,14 +16,14 @@
 PLANE = 4
 TILE = 256
 ORDER = (
-    (0, 0), (0, 1), (0, 2), (0, 3), (1, 0), (1, 1), (0, 4), (1, 3), (0, 5), (2, 1),
-    (1, 2), (0, 6), (1, 4), (0, 7), (2, 3), (3, 1), (9, 0), (1, 5), (2, 0), (3, 3),
-    (10, 1), (10, 2), (4, 1), (2, 4), (2, 2), (4, 3), (1, 6), (10, 3), (10, 4), (10, 5),
-    (2, 5), (5, 1), (3, 4), (5, 3), (1, 7), (3, 0), (3, 5), (6, 1), (10, 6), (10, 7),
-    (10, 8), (3, 2), (2, 7), (6, 3), (4, 5), (2, 6), (4, 4), (7, 1), (4, 2), (4, 0),
-    (3, 7), (7, 3), (5, 5), (3, 6), (5, 4), (10, 9), (10, 10), (5, 0), (5, 2), (6, 5),
-    (4, 7), (4, 6), (6, 4), (10, 11), (10, 12), (7, 5), (6, 0), (5, 7), (5, 6), (7, 4),
-    (6, 2), (6, 7), (10, 13), (10, 14), (10, 15), (6, 6), (7, 0), (7, 2), (7, 7), (7, 6),
+    (0, 0), (0, 1), (0, 2), (0, 3), (0, 4), (1, 0), (1, 1), (1, 3), (0, 5), (1, 2),
+    (0, 6), (1, 4), (2, 1), (0, 7), (2, 3), (2, 0), (9, 0), (10, 1), (3, 1), (3, 3),
+    (1, 5), (10, 2), (10, 3), (10, 4), (2, 4), (4, 1), (4, 3), (10, 5), (3, 4), (3, 0),
+    (2, 2), (10, 6), (1, 6), (2, 5), (5, 1), (1, 7), (5, 3), (3, 2), (3, 5), (10, 7),
+    (10, 8), (6, 1), (10, 9), (6, 3), (2, 7), (4, 5), (2, 6), (4, 0), (4, 2), (4, 4),
+    (7, 1), (5, 2), (3, 7), (5, 5), (7, 3), (3, 6), (10, 10), (5, 4), (10, 11), (4, 7),
+    (6, 5), (5, 0), (4, 6), (10, 12), (10, 13), (6, 4), (7, 5), (6, 0), (5, 6), (7, 4),
+    (5, 7), (6, 2), (10, 14), (10, 15), (6, 6), (6, 7), (7, 0), (7, 2), (7, 6), (7, 7),
     (11, 0),
 )
 PLANES_FIRST = ((2, 0), (2, 1), (0, 1))
@@ -501,7 +501,7 @@
         lax.fori_loop(0, devices, one, 0)
         strip_swap().start()
 
-    def forward(m, carry):
+    def forward(m, carry, tile=size):
         probe_load(m).wait()
 
         def leave(i, carry):
@@ -514,25 +514,20 @@
         lax.fori_loop(0, size // 64, leave, 0)
         product(left, wave)
 
-        def across(i, carry):
-            at = rows(i * TILE, TILE, TILE)
+        for i in range(size // tile):
+            at = pl.ds(i * tile, tile)
             both = jnp.dot(half[at], right[...], preferred_element_type=F32)
             re, im = both[:, :size], both[:, size:]
             far[m, 0, at] = re
             far[m, 1, at] = im
             here = re * re + im * im
             power[at] = jnp.where(m == 0, here, power[at] + here)
-
-            @pl.when(m == modes - 1)
-            def _():
+            if tile == TILE:
                 swap(i).start()
-
-            return carry
-
-        lax.fori_loop(0, size // TILE, across, 0)
         return carry
 
-    lax.fori_loop(0, modes, forward, 0)
+    lax.fori_loop(0, modes - 1, forward, 0)
+    forward(modes - 1, 0, TILE)
     for i in range(size // TILE):
         at = pl.ds(i * TILE, TILE)
         swap(i).wait_recv()

time: 126 us -> 124 us (0.984)
  Pallas kernels: 123 us -> 121 us
    pallas_call x1, Pallas kernels: 120 us -> 118 us  [shards(): pl.pallas_call(core_kernel, out_shape=(vmem((modes, 2, size, size), BF16)...]
where the time goes in v10:
time: 124 us
  Pallas kernels  121 us (98%)
  between operations  2.74 us (2%)
    pallas_call x1, Pallas kernels, shards(): pl.pallas_call(core_kernel, out_shape=(vmem((modes, 2, size, size), BF16)...  118 us
    pallas_call x1, Pallas kernels, shards(): pl.pallas_call(cast_kernel, out_shape=(jax.ShapeDtypeStruct(term.shape, F...  3.46 us

profile of v10, /device:TPU:0, one launch (start us, length us, event | category | flops | bytes accessed | tf_op | source)
XLA Modules:
  0.0 123.7 jit_solution(12855059981410402801)
XLA Ops:
  2.6 117.5 %shard_map.95 = (bf16[4,2,512,512]{3,2,1,0:T(8,128)(2,1)S(1)}, f32[2,40,1152]{2,1,0:T(8,128)S(1)}) custom-call(s32[1]{0:T(128)S(6)} %copy.12.strip_of, s32[1]{0:T(128)S(6)} %copy.10.row, s32[1]{0:T(128)S(6)} %copy.11.col, f32[2,40,1152]{2,1,0:T(8,128)} %field_hbm.1, f32[4,2,512,512]{3,2,1,0:T(8,128)} %probe_hbm.1, f32[512,512]{1,0:T(8,128)} %bitcast.1, ...), custom_call_target="tpu_custom_call" | custom-call | tf_op jit(solution)/shard_map/pallas_call | solution.py:670
  120.1 3.5 %shard_map.96 = (f32[4,2,512,512]{3,2,1,0:T(8,128)}, f32[2,40,1152]{2,1,0:T(8,128)}) custom-call(bf16[4,2,512,512]{3,2,1,0:T(8,128)(2,1)S(1)} %get-tuple-element.6.summed, f32[2,40,1152]{2,1,0:T(8,128)S(1)} %get-tuple-element.7.strips), custom_call_target="tpu_custom_call" | custom-call | tf_op jit(solution)/shard_map/pallas_call | solution.py:725

commit v11 on v10

--- a/solution.py
+++ b/solution.py
@@ -600,15 +600,21 @@
     last = pltpu.make_async_copy(strips, strip_grad, strip_done)
     last.start()
 
+    half = block.shape[1]
+    count = 2 * modes * (summed.shape[2] // half)
+
+    def at(ref, i):
+        return ref.at[i // 4, i // 2 % 2, pl.ds(i % 2 * half, half)]
+
     def out(i):
-        return pltpu.make_async_copy(block.at[i % depth], wide.at[i // 2, i % 2], done.at[i % depth])
-
-    for i in range(2 * modes):
+        return pltpu.make_async_copy(block.at[i % depth], at(wide, i), done.at[i % depth])
+
+    for i in range(count):
         if i >= depth:
             out(i - depth).wait()
-        block[i % depth] = summed[i // 2, i % 2].astype(F32)
+        block[i % depth] = at(summed, i)[...].astype(F32)
         out(i).start()
-    for i in range(max(2 * modes - depth, 0), 2 * modes):
+    for i in range(max(count - depth, 0), count):
         out(i).wait()
     last.wait()
 
@@ -727,7 +733,7 @@
             out_shape=(jax.ShapeDtypeStruct(term.shape, F32), jax.ShapeDtypeStruct(strip_grad.shape, F32)),
             in_specs=[VMEM] * 2,
             out_specs=(any_space, any_space),
-            scratch_shapes=[vmem((4, size, size), F32), dma((4,)), dma],
+            scratch_shapes=[vmem((16, size // 2, size), F32), dma((16,)), dma],
             compiler_params=pltpu.CompilerParams(vmem_limit_bytes=16 * 1024 * 1024),
         )(pltpu.with_memory_space_constraint(term, vmem), pltpu.with_memory_space_constraint(strip_grad, vmem))
         return (strip_grad, probe_grad)

time: 124 us -> 124 us (level)
  no operation moved by 1% of the time
where the time goes in v11:
time: 124 us
  Pallas kernels  121 us (98%)
  between operations  2.74 us (2%)
    pallas_call x1, Pallas kernels, shards(): pl.pallas_call(core_kernel, out_shape=(vmem((modes, 2, size, size), BF16)...  118 us
    pallas_call x1, Pallas kernels, shards(): pl.pallas_call(cast_kernel, out_shape=(jax.ShapeDtypeStruct(term.shape, F...  3.55 us

profile of v11, /device:TPU:0, one launch (start us, length us, event | category | flops | bytes accessed | tf_op | source)
XLA Modules:
  0.0 123.8 jit_solution(13236395239144816751)
XLA Ops:
  2.6 117.5 %shard_map.95 = (bf16[4,2,512,512]{3,2,1,0:T(8,128)(2,1)S(1)}, f32[2,40,1152]{2,1,0:T(8,128)S(1)}) custom-call(s32[1]{0:T(128)S(6)} %copy.12.strip_of, s32[1]{0:T(128)S(6)} %copy.10.row, s32[1]{0:T(128)S(6)} %copy.11.col, f32[2,40,1152]{2,1,0:T(8,128)} %field_hbm.1, f32[4,2,512,512]{3,2,1,0:T(8,128)} %probe_hbm.1, f32[512,512]{1,0:T(8,128)} %bitcast.1, ...), custom_call_target="tpu_custom_call" | custom-call | tf_op jit(solution)/shard_map/pallas_call | solution.py:676
  120.1 3.6 %shard_map.96 = (f32[4,2,512,512]{3,2,1,0:T(8,128)}, f32[2,40,1152]{2,1,0:T(8,128)}) custom-call(bf16[4,2,512,512]{3,2,1,0:T(8,128)(2,1)S(1)} %get-tuple-element.6.summed, f32[2,40,1152]{2,1,0:T(8,128)S(1)} %get-tuple-element.7.strips), custom_call_target="tpu_custom_call" | custom-call | tf_op jit(solution)/shard_map/pallas_call | solution.py:731
